TPU v7x, 256 devices: a whole 4x4x8 slice. The times are simulated.
256 devices in a mesh: row: 8 (over x, core), col: 32 (over z, y).
Axes of the slice: x: 4, y: 4, z: 8, core: 2. Of those that a mesh axis runs over, the one named last changes fastest.
Arguments:
- tangent: bfloat16 [32, 131072], P(None, ('col', 'row')), may hold values from -180 to 180
- activity: bfloat16 [131072], P(('col', 'row')), may hold values from -5 to 5
- block_keys: int32 [8, 512], P('row', 'col'), may hold values from 0 to 1073741823
Outputs:
- tangent_new: float32 [32, 131072], P(None, ('row', 'col'))
- next_state: float32 [131072], P(('row', 'col'))
- r_factor: float32 [32, 32], replicated
- first_factor: float32 [32, 32], replicated
All inputs are finite; a program needn't handle non-finite values.
Results may differ from a plain program's by a relative error of at most 0.0006.
Values may be sent and summed in bfloat16 or wider, within the bound.
No kernel may reach another device: no remote copies, remote signals or barrier semaphores. Data moves between devices by JAX's collectives and lax.ppermute only.
A program may use at most 64 MiB of HBM per device.

v0:
```python
import math

import jax
import jax.numpy as jnp
from jax import lax
from jax.sharding import PartitionSpec as P

N = 131072
KEYCOLS = 256


def coupling_values(tile_key, row_ids, column_ids):
    hashed = tile_key + row_ids * 374761393 + column_ids * 668265261
    hashed = hashed ^ lax.shift_right_logical(hashed, jnp.int32(15))
    hashed = hashed * 739982445
    hashed = hashed ^ lax.shift_right_logical(hashed, jnp.int32(13))
    hashed = hashed * 695872825
    hashed = hashed ^ lax.shift_right_logical(hashed, jnp.int32(16))
    return (jnp.bitwise_and(hashed, 255) - 128).astype(jnp.bfloat16)


def derivative_scaled(drive):
    coupling_scale = 2.0 / math.sqrt(5461.25 * N)
    next_state = jnp.tanh(coupling_scale * drive[-1])
    grown = (coupling_scale * (1.0 - next_state * next_state))[None, :] * drive[:-1]
    return (next_state, grown)


def orthonormalize(grown, first_sum, second_sum):
    highest = lax.Precision.HIGHEST
    gram_one = first_sum(jnp.dot(grown, grown.T, precision=highest)) / N
    lower_one = jnp.linalg.cholesky(gram_one)
    first = jax.scipy.linalg.solve_triangular(lower_one, grown, lower=True)
    gram_two = second_sum(jnp.dot(first, first.T, precision=highest)) / N
    lower_two = jnp.linalg.cholesky(gram_two)
    result = jax.scipy.linalg.solve_triangular(lower_two, first, lower=True)
    return (result, jnp.dot(lower_one, lower_two, precision=highest).T, lower_one.T)


def contract(segment, coupling):
    return lax.dot_general(
        segment, coupling, (((1,), (1,)), ((), ())), preferred_element_type=jnp.float32
    )


def per_device(tangent, activity, block_keys):
    vec_count = tangent.shape[0]
    row_count = lax.axis_size("row")
    col_count = lax.axis_size("col")
    group_rows = N // row_count
    block_columns = N // col_count
    row_ids = lax.axis_index("row") * group_rows + jnp.arange(group_rows, dtype=jnp.int32)
    column_base = lax.axis_index("col") * block_columns
    local_keys = block_keys[0]
    initial = jnp.zeros((vec_count + 1, group_rows), jnp.float32)
    vectors = jnp.concatenate(
        (
            lax.all_gather(tangent, "row", axis=1, tiled=True),
            lax.all_gather(activity.reshape(1, -1), "row", axis=1, tiled=True),
        ),
        axis=0,
    )
    tile_count = vectors.shape[1] // KEYCOLS

    def one_tile(tile_number, partial_value):
        offset = tile_number * KEYCOLS
        tile_key = lax.dynamic_index_in_dim(local_keys, offset // KEYCOLS, 0, keepdims=False)
        column_ids = column_base + offset + jnp.arange(KEYCOLS, dtype=jnp.int32)
        coupling = coupling_values(tile_key, row_ids[:, None], column_ids[None, :])
        segment = lax.dynamic_slice_in_dim(vectors, offset, KEYCOLS, 1)
        return partial_value + contract(segment, coupling)

    totals = lax.fori_loop(0, tile_count, one_tile, initial)
    own_drive = lax.psum_scatter(totals, "col", scatter_dimension=1, tiled=True)
    next_state, grown = derivative_scaled(own_drive)
    tangent_new, r_factor, first_factor = orthonormalize(
        grown,
        lambda gram: lax.psum(gram, ("row", "col")),
        lambda gram: lax.psum(gram, ("row", "col")),
    )
    return (tangent_new, next_state, r_factor, first_factor)


def solution(mesh):
    placed = (P(None, ("col", "row")), P(("col", "row")), P("row", "col"))
    return jax.shard_map(
        per_device,
        mesh=mesh,
        in_specs=placed,
        out_specs=(P(None, ("row", "col")), P(("row", "col")), P(), P()),
        check_vma=False,
    )
```

profile of v0, /device:TPU:1, one launch (start us, length us, event | category | flops | bytes accessed | tf_op | source)
XLA Modules:
  0.0 595.3 jit_solution(17989895351228089019)
XLA Ops:
  7.9 14.3 %all-gather.1 = bf16[8,1,512]{2,1,0:T(2,128)(2,1)S(1)} all-gather(bf16[1,1,512]{2,1,0:T(2,128)(2,1)S(1)} %reshape.39), channel_id=2, replica_groups=mesh['row'=8,'col'=32] {'row'}, dimensions={0}, use_global_device_ids=true | all-gather | bytes 9216 | tf_op jit(solution)/shard_map/all_gather | solution.py:59
  22.2 13.1 %all_gather.6 = bf16[32,4096]{1,0:T(8,128)(2,1)S(1)} all-gather(bf16[32,512]{1,0:T(8,128)(2,1)} %param.8), channel_id=1, replica_groups=mesh['row'=8,'col'=32] {'row'}, dimensions={1}, use_global_device_ids=true | all-gather | bytes 294912 | tf_op jit(solution)/shard_map/all_gather | solution.py:58
  35.3 163.6 %while.16 = (s32[]{:T(128)}, f32[33,16384]{1,0:T(8,128)S(1)}, bf16[33,4096]{1,0:T(8,128)(2,1)S(1)}, s32[16]{0:T(128)}, s32[]{:T(128)}, /*index=5*/s32[]{:T(128)}...) while((s32[]{:T(128)}, f32[33,16384]{1,0:T(8,128)S(1)}, ...), condition=%wide.region_1.2_spmd.clone, body=%wide.region_0.1_spmd.clone.sunk | while | flops 328286752 | bytes 4938140 | solution.py:73
  37.2 8.3 %convolution_add_fusion.2 = f32[33,16384]{1,0:T(8,128)S(1)} fusion(s32[256]{0:T(256)S(1)} %add_multiply_fusion.3, s32[16384]{0:T(1024)S(1)} %fusion.63, f32[33,16384]{1,0:T(8,128)S(1)} %get-tuple-element.263, pred[]{:T(512)S(6)} %compare.19, bf16[33,4096]{1,0:T(8,128)(2,1)S(1)} %get-tuple-element.278, s32[]{:T(128)S(6)} %select_n.57), kind=kOutput, calls=%fused_computation.4.clone.1 | convolution fusion | flops 328237056 | bytes 4871173 | tf_op jit(solution)/shard_map/while/body/eval_jaxpr/dot_general | solution.py:41
  47.5 8.3 %convolution_add_fusion.2 = f32[33,16384]{1,0:T(8,128)S(1)} fusion(s32[256]{0:T(256)S(1)} %add_multiply_fusion.3, s32[16384]{0:T(1024)S(1)} %fusion.63, f32[33,16384]{1,0:T(8,128)S(1)} %get-tuple-element.263, pred[]{:T(512)S(6)} %compare.19, bf16[33,4096]{1,0:T(8,128)(2,1)S(1)} %get-tuple-element.278, s32[]{:T(128)S(6)} %select_n.57), kind=kOutput, calls=%fused_computation.4.clone.1 | convolution fusion | flops 328237056 | bytes 4871173 | tf_op jit(solution)/shard_map/while/body/eval_jaxpr/dot_general | solution.py:41
  57.7 8.3 %convolution_add_fusion.2 = f32[33,16384]{1,0:T(8,128)S(1)} fusion(s32[256]{0:T(256)S(1)} %add_multiply_fusion.3, s32[16384]{0:T(1024)S(1)} %fusion.63, f32[33,16384]{1,0:T(8,128)S(1)} %get-tuple-element.263, pred[]{:T(512)S(6)} %compare.19, bf16[33,4096]{1,0:T(8,128)(2,1)S(1)} %get-tuple-element.278, s32[]{:T(128)S(6)} %select_n.57), kind=kOutput, calls=%fused_computation.4.clone.1 | convolution fusion | flops 328237056 | bytes 4871173 | tf_op jit(solution)/shard_map/while/body/eval_jaxpr/dot_general | solution.py:41
  67.9 8.3 %convolution_add_fusion.2 = f32[33,16384]{1,0:T(8,128)S(1)} fusion(s32[256]{0:T(256)S(1)} %add_multiply_fusion.3, s32[16384]{0:T(1024)S(1)} %fusion.63, f32[33,16384]{1,0:T(8,128)S(1)} %get-tuple-element.263, pred[]{:T(512)S(6)} %compare.19, bf16[33,4096]{1,0:T(8,128)(2,1)S(1)} %get-tuple-element.278, s32[]{:T(128)S(6)} %select_n.57), kind=kOutput, calls=%fused_computation.4.clone.1 | convolution fusion | flops 328237056 | bytes 4871173 | tf_op jit(solution)/shard_map/while/body/eval_jaxpr/dot_general | solution.py:41
  78.1 8.3 %convolution_add_fusion.2 = f32[33,16384]{1,0:T(8,128)S(1)} fusion(s32[256]{0:T(256)S(1)} %add_multiply_fusion.3, s32[16384]{0:T(1024)S(1)} %fusion.63, f32[33,16384]{1,0:T(8,128)S(1)} %get-tuple-element.263, pred[]{:T(512)S(6)} %compare.19, bf16[33,4096]{1,0:T(8,128)(2,1)S(1)} %get-tuple-element.278, s32[]{:T(128)S(6)} %select_n.57), kind=kOutput, calls=%fused_computation.4.clone.1 | convolution fusion | flops 328237056 | bytes 4871173 | tf_op jit(solution)/shard_map/while/body/eval_jaxpr/dot_general | solution.py:41
  88.4 8.3 %convolution_add_fusion.2 = f32[33,16384]{1,0:T(8,128)S(1)} fusion(s32[256]{0:T(256)S(1)} %add_multiply_fusion.3, s32[16384]{0:T(1024)S(1)} %fusion.63, f32[33,16384]{1,0:T(8,128)S(1)} %get-tuple-element.263, pred[]{:T(512)S(6)} %compare.19, bf16[33,4096]{1,0:T(8,128)(2,1)S(1)} %get-tuple-element.278, s32[]{:T(128)S(6)} %select_n.57), kind=kOutput, calls=%fused_computation.4.clone.1 | convolution fusion | flops 328237056 | bytes 4871173 | tf_op jit(solution)/shard_map/while/body/eval_jaxpr/dot_general | solution.py:41
  98.6 8.3 %convolution_add_fusion.2 = f32[33,16384]{1,0:T(8,128)S(1)} fusion(s32[256]{0:T(256)S(1)} %add_multiply_fusion.3, s32[16384]{0:T(1024)S(1)} %fusion.63, f32[33,16384]{1,0:T(8,128)S(1)} %get-tuple-element.263, pred[]{:T(512)S(6)} %compare.19, bf16[33,4096]{1,0:T(8,128)(2,1)S(1)} %get-tuple-element.278, s32[]{:T(128)S(6)} %select_n.57), kind=kOutput, calls=%fused_computation.4.clone.1 | convolution fusion | flops 328237056 | bytes 4871173 | tf_op jit(solution)/shard_map/while/body/eval_jaxpr/dot_general | solution.py:41
  108.8 8.3 %convolution_add_fusion.2 = f32[33,16384]{1,0:T(8,128)S(1)} fusion(s32[256]{0:T(256)S(1)} %add_multiply_fusion.3, s32[16384]{0:T(1024)S(1)} %fusion.63, f32[33,16384]{1,0:T(8,128)S(1)} %get-tuple-element.263, pred[]{:T(512)S(6)} %compare.19, bf16[33,4096]{1,0:T(8,128)(2,1)S(1)} %get-tuple-element.278, s32[]{:T(128)S(6)} %select_n.57), kind=kOutput, calls=%fused_computation.4.clone.1 | convolution fusion | flops 328237056 | bytes 4871173 | tf_op jit(solution)/shard_map/while/body/eval_jaxpr/dot_general | solution.py:41
  119.0 8.3 %convolution_add_fusion.2 = f32[33,16384]{1,0:T(8,128)S(1)} fusion(s32[256]{0:T(256)S(1)} %add_multiply_fusion.3, s32[16384]{0:T(1024)S(1)} %fusion.63, f32[33,16384]{1,0:T(8,128)S(1)} %get-tuple-element.263, pred[]{:T(512)S(6)} %compare.19, bf16[33,4096]{1,0:T(8,128)(2,1)S(1)} %get-tuple-element.278, s32[]{:T(128)S(6)} %select_n.57), kind=kOutput, calls=%fused_computation.4.clone.1 | convolution fusion | flops 328237056 | bytes 4871173 | tf_op jit(solution)/shard_map/while/body/eval_jaxpr/dot_general | solution.py:41
  129.3 8.3 %convolution_add_fusion.2 = f32[33,16384]{1,0:T(8,128)S(1)} fusion(s32[256]{0:T(256)S(1)} %add_multiply_fusion.3, s32[16384]{0:T(1024)S(1)} %fusion.63, f32[33,16384]{1,0:T(8,128)S(1)} %get-tuple-element.263, pred[]{:T(512)S(6)} %compare.19, bf16[33,4096]{1,0:T(8,128)(2,1)S(1)} %get-tuple-element.278, s32[]{:T(128)S(6)} %select_n.57), kind=kOutput, calls=%fused_computation.4.clone.1 | convolution fusion | flops 328237056 | bytes 4871173 | tf_op jit(solution)/shard_map/while/body/eval_jaxpr/dot_general | solution.py:41
  139.5 8.3 %convolution_add_fusion.2 = f32[33,16384]{1,0:T(8,128)S(1)} fusion(s32[256]{0:T(256)S(1)} %add_multiply_fusion.3, s32[16384]{0:T(1024)S(1)} %fusion.63, f32[33,16384]{1,0:T(8,128)S(1)} %get-tuple-element.263, pred[]{:T(512)S(6)} %compare.19, bf16[33,4096]{1,0:T(8,128)(2,1)S(1)} %get-tuple-element.278, s32[]{:T(128)S(6)} %select_n.57), kind=kOutput, calls=%fused_computation.4.clone.1 | convolution fusion | flops 328237056 | bytes 4871173 | tf_op jit(solution)/shard_map/while/body/eval_jaxpr/dot_general | solution.py:41
  149.7 8.3 %convolution_add_fusion.2 = f32[33,16384]{1,0:T(8,128)S(1)} fusion(s32[256]{0:T(256)S(1)} %add_multiply_fusion.3, s32[16384]{0:T(1024)S(1)} %fusion.63, f32[33,16384]{1,0:T(8,128)S(1)} %get-tuple-element.263, pred[]{:T(512)S(6)} %compare.19, bf16[33,4096]{1,0:T(8,128)(2,1)S(1)} %get-tuple-element.278, s32[]{:T(128)S(6)} %select_n.57), kind=kOutput, calls=%fused_computation.4.clone.1 | convolution fusion | flops 328237056 | bytes 4871173 | tf_op jit(solution)/shard_map/while/body/eval_jaxpr/dot_general | solution.py:41
  159.9 8.3 %convolution_add_fusion.2 = f32[33,16384]{1,0:T(8,128)S(1)} fusion(s32[256]{0:T(256)S(1)} %add_multiply_fusion.3, s32[16384]{0:T(1024)S(1)} %fusion.63, f32[33,16384]{1,0:T(8,128)S(1)} %get-tuple-element.263, pred[]{:T(512)S(6)} %compare.19, bf16[33,4096]{1,0:T(8,128)(2,1)S(1)} %get-tuple-element.278, s32[]{:T(128)S(6)} %select_n.57), kind=kOutput, calls=%fused_computation.4.clone.1 | convolution fusion | flops 328237056 | bytes 4871173 | tf_op jit(solution)/shard_map/while/body/eval_jaxpr/dot_general | solution.py:41
  170.2 8.3 %convolution_add_fusion.2 = f32[33,16384]{1,0:T(8,128)S(1)} fusion(s32[256]{0:T(256)S(1)} %add_multiply_fusion.3, s32[16384]{0:T(1024)S(1)} %fusion.63, f32[33,16384]{1,0:T(8,128)S(1)} %get-tuple-element.263, pred[]{:T(512)S(6)} %compare.19, bf16[33,4096]{1,0:T(8,128)(2,1)S(1)} %get-tuple-element.278, s32[]{:T(128)S(6)} %select_n.57), kind=kOutput, calls=%fused_computation.4.clone.1 | convolution fusion | flops 328237056 | bytes 4871173 | tf_op jit(solution)/shard_map/while/body/eval_jaxpr/dot_general | solution.py:41
  180.4 8.3 %convolution_add_fusion.2 = f32[33,16384]{1,0:T(8,128)S(1)} fusion(s32[256]{0:T(256)S(1)} %add_multiply_fusion.3, s32[16384]{0:T(1024)S(1)} %fusion.63, f32[33,16384]{1,0:T(8,128)S(1)} %get-tuple-element.263, pred[]{:T(512)S(6)} %compare.19, bf16[33,4096]{1,0:T(8,128)(2,1)S(1)} %get-tuple-element.278, s32[]{:T(128)S(6)} %select_n.57), kind=kOutput, calls=%fused_computation.4.clone.1 | convolution fusion | flops 328237056 | bytes 4871173 | tf_op jit(solution)/shard_map/while/body/eval_jaxpr/dot_general | solution.py:41
  190.6 8.3 %convolution_add_fusion.2 = f32[33,16384]{1,0:T(8,128)S(1)} fusion(s32[256]{0:T(256)S(1)} %add_multiply_fusion.3, s32[16384]{0:T(1024)S(1)} %fusion.63, f32[33,16384]{1,0:T(8,128)S(1)} %get-tuple-element.263, pred[]{:T(512)S(6)} %compare.19, bf16[33,4096]{1,0:T(8,128)(2,1)S(1)} %get-tuple-element.278, s32[]{:T(128)S(6)} %select_n.57), kind=kOutput, calls=%fused_computation.4.clone.1 | convolution fusion | flops 328237056 | bytes 4871173 | tf_op jit(solution)/shard_map/while/body/eval_jaxpr/dot_general | solution.py:41
  200.4 213.8 %reduce-scatter.2.cloned.1.call-done = f32[33,512]{1,0:T(8,128)} async-done(((f32[33,16384]{1,0:T(8,128)}), f32[33,512]{1,0:T(8,128)}) %reduce-scatter.2.cloned.1.call-update) | async-done | bytes 67600 | tf_op jit(solution)/shard_map/reduce_scatter | solution.py:74
  416.7 79.6 %psum.14 = f32[32,32]{0,1:T(8,128)S(1)} all-reduce(f32[32,32]{0,1:T(8,128)S(1)} %fusion.28), channel_id=1, replica_groups=mesh['row'=8,'col'=32] {'row','col'}, use_global_device_ids=true, to_apply=%region_3.4 | all-reduce | flops 1024 | bytes 8192 | tf_op jit(solution)/shard_map/psum | solution.py:78
  496.3 2.9 cholesky.44
  504.4 73.7 %psum.15 = f32[32,32]{0,1:T(8,128)S(1)} all-reduce(f32[32,32]{0,1:T(8,128)S(1)} %fusion.54), channel_id=1, replica_groups=mesh['row'=8,'col'=32] {'row','col'}, use_global_device_ids=true, to_apply=%region_6.9 | all-reduce | flops 1024 | bytes 8192 | tf_op jit(solution)/shard_map/psum | solution.py:79
  578.1 2.9 cholesky.55
  (76 shorter events, 47.8 us)
Async XLA Ops:
  7.2 407.1 %reduce-scatter.2.cloned.1.call-start = ((), (), s32[]{:S(2)}) async-start(), calls=%async_computation.1 | async-start | bytes 2703360 | tf_op jit(solution)/shard_map/reduce_scatter | solution.py:74
  198.9 1.5 copy-start
Sparse Core Ops, SparseCore 0:
  200.6 213.6 reduce-scatter.1
where the time goes:
time: 596 us; the launch traced here: 595 us
  waiting for transfers between devices  214 us (36%)
  blocking collectives  181 us (30%)
  matrix products  138 us (23%)
  other arithmetic  25.3 us (4%)
  local copies, waits for them, and re-layouts  22.9 us (4%)
  between operations  14.1 us (2%)
    reduce_scatter x1, waiting for transfers between devices, per_device(): own_drive = lax.psum_scatter(totals, 'col', scatter_dimension=1, tiled=True)  214 us
    psum x2, blocking collectives, per_device(): lax.psum(gram, ('row', 'col'))  153 us
    dot_general x16, matrix products, contract(): lax.dot_general(segment, coupling, (((1,), (1,)), ((), ())), preferred_el...  132 us
    dynamic_slice x16, local copies, waits for them, and re-layouts, one_tile(): lax.dynamic_index_in_dim(local_keys, offset // KEYCOLS, 0, keepdims=False)  19.9 us
    all_gather x1, blocking collectives, per_device(): lax.all_gather(activity.reshape(1, -1), 'row', axis=1, tiled=True)  14.3 us
    all_gather x1, blocking collectives, per_device(): lax.all_gather(tangent, 'row', axis=1, tiled=True)  13.1 us
  transfers between devices with their start and end apart: 1, of which 1 were waited for; matrix products, arithmetic and copies ran while one was open for 0% of the time, Pallas kernels for 0%

commit v1 on v0

v1 whole, which is shorter than its diff:
```python
import functools
import math

import jax
import jax.numpy as jnp
from jax import lax
from jax.experimental import pallas as pl
from jax.experimental.pallas import tpu as pltpu
from jax.sharding import Mesh
from jax.sharding import PartitionSpec as P

N = 131072
VECS = 32
PAD = 48
KEYCOLS = 256
X, CORE, Z, Y = 4, 2, 8, 4
OWN = N // (X * CORE * Z * Y)
ROWS = OWN * Y
SEG = OWN * X * CORE
GROUP = 32
SCALE = 2.0 / math.sqrt(5461.25 * N)
HIGH = lax.Precision.HIGHEST
VMEM_LIMIT = 48 * 2**20


def shift_right(value, amount):
    return lax.shift_right_logical(value, jnp.full(value.shape, amount, jnp.int32))


def coupling(value):
    value = value ^ shift_right(value, 15)
    value = value * jnp.int32(739982445)
    value = value ^ shift_right(value, 13)
    value = value * jnp.int32(695872825)
    value = value ^ shift_right(value, 16)
    return (value.astype(jnp.int8) ^ jnp.int8(-128)).astype(jnp.bfloat16)


def drive_kernel(rows_ref, bases_ref, vectors_ref, out_ref, *, segments, step):
    spread = lax.broadcasted_iota(jnp.int32, (GROUP, 128), 0) * jnp.int32(668265261)
    left = rows_ref[:, :128] + spread
    right = rows_ref[:, 128:] + spread
    groups = step * SEG // GROUP

    def body(number, total):
        first = pl.multiple_of(number * groups, groups)
        parts = []
        for group in range(groups):
            base = bases_ref[pl.ds(first + group, 1), :]
            parts.append(jnp.concatenate((coupling(base + left), coupling(base + right)), axis=1))
        vectors = jnp.concatenate([vectors_ref[number * step + k] for k in range(step)], axis=1)
        return total + jnp.dot(
            vectors, jnp.concatenate(parts, axis=0), preferred_element_type=jnp.float32
        )

    out_ref[...] = lax.fori_loop(
        0, segments // step, body, jnp.zeros(out_ref.shape, jnp.float32)
    )


def partial_drive(row_terms, bases, vectors, step):
    segments = vectors.shape[0]
    return pl.pallas_call(
        functools.partial(drive_kernel, segments=segments, step=step),
        grid=(row_terms.shape[1] // 256,),
        in_specs=[
            pl.BlockSpec((1, 256), lambda i: (0, i)),
            pl.BlockSpec(bases.shape, lambda i: (0, 0)),
            pl.BlockSpec(vectors.shape, lambda i: (0, 0, 0)),
        ],
        out_specs=pl.BlockSpec((PAD, 256), lambda i: (0, i)),
        out_shape=jax.ShapeDtypeStruct((PAD, row_terms.shape[1]), jnp.float32),
        compiler_params=pltpu.CompilerParams(vmem_limit_bytes=VMEM_LIMIT),
    )(row_terms, bases, vectors)


def pack_gram(gram):
    return jnp.concatenate([gram[8 * k : 8 * k + 8] for k in range(4)], axis=1)


def unpack_gram(packed):
    return jnp.concatenate([packed[:, 32 * k : 32 * k + 32] for k in range(4)], axis=0)


def gram_of(rows):
    return lax.dot_general(
        rows, rows, (((1,), (1,)), ((), ())), precision=HIGH, preferred_element_type=jnp.float32
    ) / N


def factor(gram):
    rows = lax.broadcasted_iota(jnp.int32, (VECS, VECS), 0)
    columns = lax.broadcasted_iota(jnp.int32, (VECS, VECS), 1)
    work = jnp.concatenate((gram, (rows == columns).astype(jnp.float32)), axis=1)
    row_at = lax.broadcasted_iota(jnp.int32, (VECS, 1), 0)
    scales = jnp.zeros((VECS, 1), jnp.float32)
    for j in range(VECS):
        pivot_row = work[j : j + 1, :]
        pivot = work[j : j + 1, j : j + 1]
        ratio = jnp.where(row_at > j, work[:, j : j + 1] / pivot, 0.0)
        scales = jnp.where(row_at == j, lax.rsqrt(pivot), scales)
        work = work - ratio * pivot_row
    work = work * scales
    upper = jnp.where(rows <= columns, work[:, :VECS], 0.0)
    return upper, work[:, VECS:]


def first_kernel(pieces_ref, state_ref, grown_ref, gram_ref):
    drive = pieces_ref[0] + pieces_ref[1] + pieces_ref[2] + pieces_ref[3]
    state = jnp.tanh(SCALE * drive[VECS : VECS + 1])
    grown = (SCALE * (1.0 - state * state)) * drive[:VECS]
    state_ref[...] = state
    grown_ref[...] = grown
    gram_ref[...] = pack_gram(gram_of(grown))


def second_kernel(grams_ref, grown_ref, first_ref, gram_ref, upper_ref):
    upper, inverse = factor(unpack_gram(jnp.sum(grams_ref[...], axis=0)))
    first = jnp.dot(inverse, grown_ref[...], precision=HIGH, preferred_element_type=jnp.float32)
    first_ref[...] = first
    upper_ref[...] = upper
    gram_ref[...] = pack_gram(gram_of(first))


def third_kernel(grams_ref, first_ref, upper_ref, result_ref, product_ref):
    upper, inverse = factor(unpack_gram(jnp.sum(grams_ref[...], axis=0)))
    result_ref[...] = jnp.dot(
        inverse, first_ref[...], precision=HIGH, preferred_element_type=jnp.float32
    )
    product_ref[...] = jnp.dot(
        upper, upper_ref[...], precision=HIGH, preferred_element_type=jnp.float32
    )


def spread_to(value, axes, count):
    return lax.all_to_all(jnp.broadcast_to(value, (count, *value.shape)), axes, 0, 0)


def gather_grams(gram):
    near = jnp.sum(spread_to(gram, ("x", "core"), X * CORE), axis=0)
    return spread_to(near, ("z", "y"), Z * Y)


def per_device(tangent, activity, block_keys):
    group = lax.axis_index("x") * CORE + lax.axis_index("core")
    z, y = lax.axis_index("z"), lax.axis_index("y")
    own = jnp.concatenate(
        (tangent, activity.reshape(1, -1), jnp.zeros((PAD - VECS - 1, OWN), jnp.bfloat16)), axis=0
    )
    vectors = lax.all_gather(own, ("x", "core"), axis=1, tiled=True)
    vectors = lax.all_gather(vectors, "z")
    keys = lax.all_gather(block_keys[0], "z")
    columns = (jnp.arange(Z, dtype=jnp.int32)[:, None] * Y + y) * SEG + jnp.arange(
        0, SEG, GROUP, dtype=jnp.int32
    )[None, :]
    bases = jnp.repeat(keys, KEYCOLS // GROUP, axis=1) + columns * 668265261
    bases = jnp.broadcast_to(bases.reshape(-1, 1), (bases.size, 128))
    row_ids = group * (N // (X * CORE)) + z * ROWS + jnp.arange(ROWS, dtype=jnp.int32)
    partial = partial_drive((row_ids * 374761393).reshape(1, ROWS), bases, vectors, 2)

    pieces = []
    for shift in range(Y):
        to = (y + shift) % Y
        piece = lax.dynamic_slice_in_dim(partial, to * OWN, OWN, 1)
        if shift:
            piece = lax.ppermute(piece, "y", [(i, (i + shift) % Y) for i in range(Y)])
        pieces.append(piece)

    state, grown, gram = pl.pallas_call(
        first_kernel,
        out_shape=(
            jax.ShapeDtypeStruct((1, OWN), jnp.float32),
            jax.ShapeDtypeStruct((VECS, OWN), jnp.float32),
            jax.ShapeDtypeStruct((8, 128), jnp.float32),
        ),
    )(jnp.stack(pieces))
    first, gram, upper = pl.pallas_call(
        second_kernel,
        out_shape=(
            jax.ShapeDtypeStruct((VECS, OWN), jnp.float32),
            jax.ShapeDtypeStruct((8, 128), jnp.float32),
            jax.ShapeDtypeStruct((VECS, VECS), jnp.float32),
        ),
    )(gather_grams(gram), grown)
    result, product = pl.pallas_call(
        third_kernel,
        out_shape=(
            jax.ShapeDtypeStruct((VECS, OWN), jnp.float32),
            jax.ShapeDtypeStruct((VECS, VECS), jnp.float32),
        ),
    )(gather_grams(gram), first, upper)
    return result, state.reshape(OWN), product, upper


def solution(mesh):
    split = Mesh(mesh.devices.reshape(X, CORE, Z, Y), ("x", "core", "z", "y"))
    columns, rows = ("z", "y", "x", "core"), ("x", "core", "z", "y")
    return jax.shard_map(
        per_device,
        mesh=split,
        in_specs=(P(None, columns), P(columns), P(("x", "core"), ("z", "y"))),
        out_specs=(P(None, rows), P(rows), P(), P()),
        check_vma=False,
    )
```

time: 596 us -> 247 us (0.41)
  waiting for transfers between devices: 214 us -> 37.3 us
  matrix products: 138 us -> 0 us
  Pallas kernels: 0 us -> 107 us
  blocking collectives: 181 us -> 77.8 us
  other arithmetic: 25.3 us -> 1.72 us
  local copies, waits for them, and re-layouts: 22.9 us -> 4.45 us
    reduce_scatter x1 -> x0, waiting for transfers between devices: 214 us -> none  [per_device(): own_drive = lax.psum_scatter(totals, 'col', scatter_dimension=1, tiled=True)]
    psum x2 -> x0, blocking collectives: 153 us -> none  [per_device(): lax.psum(gram, ('row', 'col'))]
    dot_general x19 -> x0, matrix products: 136 us -> none  [the longest x16 132 us: contract(): lax.dot_general(segment, coupling, (((1,), (1,)), ((), ())), preferred_el...]
    pallas_call x0 -> x4, Pallas kernels: none -> 107 us  [the longest x1 95.8 us: partial_drive(): pl.pallas_call(functools.partial(drive_kernel, segments=segments, step=st...]
    all_to_all x0 -> x4, blocking collectives: none -> 46.5 us  [spread_to(): lax.all_to_all(jnp.broadcast_to(value, (count, *value.shape)), axes, 0, 0)]
    all_gather x0 -> x1, waiting for transfers between devices: none -> 31 us  [per_device(): vectors = lax.all_gather(vectors, 'z')]
    dynamic_slice x16 -> x0, local copies, waits for them, and re-layouts: 19.9 us -> none  [one_tile(): lax.dynamic_index_in_dim(local_keys, offset // KEYCOLS, 0, keepdims=False)]
    another operation x9 -> x1, other arithmetic: 12.7 us -> 0.77 us  [per_device(): jnp.stack(pieces)]
  transfers between devices with their start and end apart: 1 -> 4, of which waited for: 1 -> 4; matrix products, arithmetic and copies ran while one was open for 0% -> 0% of each run, Pallas kernels for 0% -> 0%
where the time goes in v1:
time: 247 us; the launch traced here: 246 us
  Pallas kernels  107 us (43%)
  blocking collectives  77.8 us (31%)
  waiting for transfers between devices  37.3 us (15%)
  between operations  14.2 us (6%)
  local copies, waits for them, and re-layouts  4.45 us (2%)
  starting transfers between devices  3.71 us (2%)
    pallas_call x1, Pallas kernels, partial_drive(): pl.pallas_call(functools.partial(drive_kernel, segments=segments, step=st...  95.8 us
    all_to_all x4, blocking collectives, spread_to(): lax.all_to_all(jnp.broadcast_to(value, (count, *value.shape)), axes, 0, 0)  46.5 us
    all_gather x1, waiting for transfers between devices, per_device(): vectors = lax.all_gather(vectors, 'z')  31 us
    all_gather x1, blocking collectives, per_device(): vectors = lax.all_gather(own, ('x', 'core'), axis=1, tiled=True)  17.2 us
    all_gather x1, blocking collectives, per_device(): keys = lax.all_gather(block_keys[0], 'z')  14.1 us
    ppermute x3, waiting for transfers between devices, per_device(): piece = lax.ppermute(piece, 'y', [(i, (i + shift) % Y) for i in range(Y)])  6.33 us
  transfers between devices with their start and end apart: 4, of which 4 were waited for; matrix products, arithmetic and copies ran while one was open for 0% of the time, Pallas kernels for 0%

profile of v1, /device:TPU:1, one launch (start us, length us, event | category | flops | bytes accessed | tf_op | source)
XLA Modules:
  0.0 246.3 jit_solution(16136748468709834338)
XLA Ops:
  7.2 0.7 reshape.65
  8.0 0.8 maximum_maximum_fusion
  8.8 17.2 %all_gather.13 = bf16[48,4096]{1,0:T(8,128)(2,1)} all-gather(bf16[48,512]{1,0:T(8,128)(2,1)S(1)} %maximum_maximum_fusion), channel_id=1, replica_groups=mesh['x'=4,'core'=2,'z'=8,'y'=4] {'x','core'}, dimensions={1}, use_global_device_ids=true | all-gather | bytes 442368 | tf_op jit(solution)/shard_map/all_gather | solution.py:150
  26.1 14.1 %all-gather.1 = s32[8,1,16]{2,1,0:T(1,128)S(1)} all-gather(s32[1,1,16]{2,1,0:T(1,128)} %bitcast.16), channel_id=1, replica_groups=mesh['x'=4,'core'=2,'z'=8,'y'=4] {'z'}, dimensions={0}, use_global_device_ids=true | all-gather | bytes 576 | tf_op jit(solution)/shard_map/all_gather | solution.py:152
  40.4 31.0 %all-gather.4.cloned.1.call-done = bf16[384,4096]{1,0:T(8,128)(2,1)} async-done(((bf16[48,4096]{1,0:T(8,128)(2,1)}), bf16[384,4096]{1,0:T(8,128)(2,1)}) %all-gather.4.cloned.1.call-update) | async-done | bytes 3145744 | tf_op jit(solution)/shard_map/all_gather | solution.py:151
  71.4 0.2 broadcast_in_dim.26.bases_ref
  71.6 1.9 copy-done
  73.5 95.8 %shard_map.66 = f32[48,2048]{1,0:T(8,128)S(1)} custom-call(s32[1,2048]{1,0:T(1,128)S(1)} %add_multiply_fusion.rows_ref, s32[1024,128]{1,0:T(8,128)S(1)} %broadcast_in_dim.26.bases_ref, bf16[8,48,4096]{2,1,0:T(8,128)(2,1)S(1)} %bitcast.11), custom_call_target="tpu_custom_call" | custom-call | tf_op jit(solution)/shard_map/pallas_call | solution.py:63
  169.3 2.5 %collective-permute-start.2 = (f32[48,512]{1,0:T(8,128)S(1)}, f32[48,512]{1,0:T(8,128)S(1)}, u32[]{:S(2)}, u32[]{:S(2)}) collective-permute-start(f32[48,512]{1,0:T(8,128)S(1)} %get-tuple-element.21), channel_id=1, source_target_pairs={{0,3},{1,0},{2,1},{3,2},{4,7},{5,4},{6,5},{7,6},{8,11},{9,8},{10,9... | collective-permute-start | bytes 294920 | tf_op jit(solution)/shard_map/ppermute | solution.py:166
  171.9 0.5 collective-permute-start.1
  172.4 0.6 collective-permute-start
  173.0 0.5 collective-permute-done.2
  173.5 3.4 %collective-permute-done.1 = f32[48,512]{1,0:T(8,128)S(1)} collective-permute-done((f32[48,512]{1,0:T(8,128)S(1)}, f32[48,512]{1,0:T(8,128)S(1)}, u32[]{:S(2)}, u32[]{:S(2)}) %collective-permute-start.1) | collective-permute-done | bytes 98336 | tf_op jit(solution)/shard_map/ppermute | solution.py:166
  176.9 2.4 collective-permute-done
  179.3 0.8 pad_maximum_fusion.pieces_ref
  180.1 1.9 shard_map.67
  182.0 0.7 broadcast_in_dim.28
  182.7 10.1 %all_to_all.20 = f32[8,8,128]{2,1,0:T(8,128)S(1)} all-to-all(f32[8,8,128]{2,1,0:T(8,128)S(1)} %broadcast_in_dim.28), channel_id=1, replica_groups=mesh['x'=4,'core'=2,'z'=8,'y'=4] {'x','core'}, dimensions={0} | all-to-all | bytes 65536 | tf_op jit(solution)/shard_map/all_to_all | solution.py:136
  192.8 14.1 %all_to_all.21.grams_ref = f32[32,8,128]{2,1,0:T(8,128)} all-to-all(f32[32,8,128]{2,1,0:T(8,128)S(1)} %broadcast_in_dim.29), channel_id=1, replica_groups=mesh['x'=4,'core'=2,'z'=8,'y'=4] {'z','y'}, dimensions={0} | all-to-all | bytes 262144 | tf_op jit(solution)/shard_map/all_to_all | solution.py:136
  206.9 4.8 %shard_map.68 = (f32[32,512]{1,0:T(8,128)}, f32[8,128]{1,0:T(8,128)}, f32[32,32]{1,0:T(8,128)}) custom-call(f32[32,8,128]{2,1,0:T(8,128)} %all_to_all.21.grams_ref, f32[32,512]{1,0:T(8,128)} %get-tuple-element.13.grown_ref), custom_call_target="tpu_custom_call" | custom-call | tf_op jit(solution)/shard_map/pallas_call | solution.py:177
  211.7 0.7 broadcast_in_dim.30
  212.4 9.2 %all_to_all.22 = f32[8,8,128]{2,1,0:T(8,128)S(1)} all-to-all(f32[8,8,128]{2,1,0:T(8,128)S(1)} %broadcast_in_dim.30), channel_id=1, replica_groups=mesh['x'=4,'core'=2,'z'=8,'y'=4] {'x','core'}, dimensions={0} | all-to-all | bytes 65536 | tf_op jit(solution)/shard_map/all_to_all | solution.py:136
  221.7 13.1 %all_to_all.23.grams_ref = f32[32,8,128]{2,1,0:T(8,128)} all-to-all(f32[32,8,128]{2,1,0:T(8,128)S(1)} %broadcast_in_dim.31), channel_id=1, replica_groups=mesh['x'=4,'core'=2,'z'=8,'y'=4] {'z','y'}, dimensions={0} | all-to-all | bytes 262144 | tf_op jit(solution)/shard_map/all_to_all | solution.py:136
  234.8 4.6 %shard_map.69 = (f32[32,512]{1,0:T(8,128)}, f32[32,32]{1,0:T(8,128)}) custom-call(f32[32,8,128]{2,1,0:T(8,128)} %all_to_all.23.grams_ref, f32[32,512]{1,0:T(8,128)} %get-tuple-element.15.first_ref, f32[32,32]{1,0:T(8,128)} %get-tuple-element.11.upper_ref), custom_call_target="tpu_custom_call" | custom-call | tf_op jit(solution)/shard_map/pallas_call | solution.py:185
  (16 shorter events, 0.5 us)
Async XLA Ops:
  7.2 64.2 %all-gather.4.cloned.1.call-start = ((), (), s32[]{:S(2)}) async-start(), calls=%async_computation.4 | async-start | bytes 3538944 | tf_op jit(solution)/shard_map/all_gather | solution.py:151
  71.6 1.9 copy-start
  169.3 4.2 %collective-permute-start.2 = (f32[48,512]{1,0:T(8,128)S(1)}, f32[48,512]{1,0:T(8,128)S(1)}, u32[]{:S(2)}, u32[]{:S(2)}) collective-permute-start(f32[48,512]{1,0:T(8,128)S(1)} %get-tuple-element.21), channel_id=1, source_target_pairs={{0,3},{1,0},{2,1},{3,2},{4,7},{5,4},{6,5},{7,6},{8,11},{9,8},{10,9... | collective-permute-start | bytes 294920 | tf_op jit(solution)/shard_map/ppermute | solution.py:166
  171.9 5.1 %collective-permute-start.1 = (f32[48,512]{1,0:T(8,128)S(1)}, f32[48,512]{1,0:T(8,128)S(1)}, u32[]{:S(2)}, u32[]{:S(2)}) collective-permute-start(f32[48,512]{1,0:T(8,128)S(1)} %get-tuple-element.22), channel_id=1, source_target_pairs={{0,2},{1,3},{2,0},{3,1},{4,6},{5,7},{6,4},{7,5},{8,10},{9,11},{10,... | collective-permute-start | bytes 294920 | tf_op jit(solution)/shard_map/ppermute | solution.py:166
  172.4 6.9 %collective-permute-start = (f32[48,512]{1,0:T(8,128)S(1)}, f32[48,512]{1,0:T(8,128)S(1)}, u32[]{:S(2)}, u32[]{:S(2)}) collective-permute-start(f32[48,512]{1,0:T(8,128)S(1)} %get-tuple-element.23), channel_id=1, source_target_pairs={{0,1},{1,2},{2,3},{3,0},{4,5},{5,6},{6,7},{7,4},{8,9},{9,10},{10,1... | collective-permute-start | bytes 294920 | tf_op jit(solution)/shard_map/ppermute | solution.py:166
Sparse Core Ops, SparseCore 0:
  26.1 45.2 all-gather.3

commit v2 on v1

--- a/solution.py
+++ b/solution.py
@@ -18,6 +18,8 @@
 ROWS = OWN * Y
 SEG = OWN * X * CORE
 GROUP = 32
+LANES = 512
+KEYS = SEG // KEYCOLS
 SCALE = 2.0 / math.sqrt(5461.25 * N)
 HIGH = lax.Precision.HIGHEST
 VMEM_LIMIT = 48 * 2**20
@@ -36,42 +38,56 @@
     return (value.astype(jnp.int8) ^ jnp.int8(-128)).astype(jnp.bfloat16)
 
 
-def drive_kernel(rows_ref, bases_ref, vectors_ref, out_ref, *, segments, step):
+def drive_kernel(places_ref, rows_ref, bases_ref, vectors_ref, *refs, segments):
+    out_ref = refs[-1]
     spread = lax.broadcasted_iota(jnp.int32, (GROUP, 128), 0) * jnp.int32(668265261)
-    left = rows_ref[:, :128] + spread
-    right = rows_ref[:, 128:] + spread
-    groups = step * SEG // GROUP
+    starts = [rows_ref[:, 128 * k : 128 * k + 128] + spread for k in range(LANES // 128)]
+    groups = SEG // GROUP
 
     def body(number, total):
-        first = pl.multiple_of(number * groups, groups)
+        place = places_ref[number]
+        first = pl.multiple_of(place * groups, groups)
         parts = []
         for group in range(groups):
             base = bases_ref[pl.ds(first + group, 1), :]
-            parts.append(jnp.concatenate((coupling(base + left), coupling(base + right)), axis=1))
-        vectors = jnp.concatenate([vectors_ref[number * step + k] for k in range(step)], axis=1)
+            parts.append(jnp.concatenate([coupling(base + start) for start in starts], axis=1))
         return total + jnp.dot(
-            vectors, jnp.concatenate(parts, axis=0), preferred_element_type=jnp.float32
+            vectors_ref[place],
+            jnp.concatenate(parts, axis=0),
+            preferred_element_type=jnp.float32,
         )
 
-    out_ref[...] = lax.fori_loop(
-        0, segments // step, body, jnp.zeros(out_ref.shape, jnp.float32)
-    )
-
-
-def partial_drive(row_terms, bases, vectors, step):
-    segments = vectors.shape[0]
+    initial = refs[0][...] if len(refs) > 1 else jnp.zeros(out_ref.shape, jnp.float32)
+    out_ref[...] = lax.fori_loop(0, segments, body, initial)
+
+
+def partial_drive(places, row_terms, bases, vectors, earlier=()):
+    segments = places.shape[0]
+    lanes = pl.BlockSpec((PAD, LANES), lambda i: (0, i))
+    hashes = segments * SEG * ROWS
     return pl.pallas_call(
-        functools.partial(drive_kernel, segments=segments, step=step),
-        grid=(row_terms.shape[1] // 256,),
+        functools.partial(drive_kernel, segments=segments),
+        grid=(ROWS // LANES,),
         in_specs=[
-            pl.BlockSpec((1, 256), lambda i: (0, i)),
+            pl.BlockSpec(memory_space=pltpu.SMEM),
+            pl.BlockSpec((1, LANES), lambda i: (0, i)),
             pl.BlockSpec(bases.shape, lambda i: (0, 0)),
             pl.BlockSpec(vectors.shape, lambda i: (0, 0, 0)),
-        ],
-        out_specs=pl.BlockSpec((PAD, 256), lambda i: (0, i)),
-        out_shape=jax.ShapeDtypeStruct((PAD, row_terms.shape[1]), jnp.float32),
+        ]
+        + [lanes] * len(earlier),
+        out_specs=lanes,
+        out_shape=jax.ShapeDtypeStruct((PAD, ROWS), jnp.float32),
+        cost_estimate=pl.CostEstimate(
+            flops=hashes * 1500, bytes_accessed=vectors.size * 2, transcendentals=0
+        ),
         compiler_params=pltpu.CompilerParams(vmem_limit_bytes=VMEM_LIMIT),
-    )(row_terms, bases, vectors)
+    )(places, row_terms, bases, vectors, *earlier)
+
+
+def base_values(keys, places, y):
+    columns = (places[:, None] * Y + y) * SEG + jnp.arange(0, SEG, GROUP, dtype=jnp.int32)[None, :]
+    values = jnp.repeat(keys, KEYCOLS // GROUP, axis=1) + columns * 668265261
+    return jnp.broadcast_to(values.reshape(-1, 1), (values.size, 128))
 
 
 def pack_gram(gram):
@@ -144,19 +160,30 @@
 def per_device(tangent, activity, block_keys):
     group = lax.axis_index("x") * CORE + lax.axis_index("core")
     z, y = lax.axis_index("z"), lax.axis_index("y")
+    keys = block_keys[0]
+    digits = [jnp.bitwise_and(shift_right(keys, 8 * k), 255).astype(jnp.bfloat16) for k in range(4)]
+    digits = jnp.concatenate(digits + [jnp.zeros(OWN - 4 * KEYS, jnp.bfloat16)])
     own = jnp.concatenate(
-        (tangent, activity.reshape(1, -1), jnp.zeros((PAD - VECS - 1, OWN), jnp.bfloat16)), axis=0
-    )
-    vectors = lax.all_gather(own, ("x", "core"), axis=1, tiled=True)
-    vectors = lax.all_gather(vectors, "z")
-    keys = lax.all_gather(block_keys[0], "z")
-    columns = (jnp.arange(Z, dtype=jnp.int32)[:, None] * Y + y) * SEG + jnp.arange(
-        0, SEG, GROUP, dtype=jnp.int32
-    )[None, :]
-    bases = jnp.repeat(keys, KEYCOLS // GROUP, axis=1) + columns * 668265261
-    bases = jnp.broadcast_to(bases.reshape(-1, 1), (bases.size, 128))
+        (
+            tangent,
+            activity.reshape(1, -1),
+            digits.reshape(1, -1),
+            jnp.zeros((PAD - VECS - 2, OWN), jnp.bfloat16),
+        ),
+        axis=0,
+    )
+    near = lax.all_gather(own, ("x", "core"), axis=1, tiled=True)
+    vectors = lax.all_gather(near, "z")
     row_ids = group * (N // (X * CORE)) + z * ROWS + jnp.arange(ROWS, dtype=jnp.int32)
-    partial = partial_drive((row_ids * 374761393).reshape(1, ROWS), bases, vectors, 2)
+    row_terms = (row_ids * 374761393).reshape(1, ROWS)
+    here = base_values(keys[None], z[None], y)
+    partial = partial_drive(jnp.zeros(1, jnp.int32), row_terms, here, near[None])
+    digits = lax.dynamic_slice(vectors, (0, VECS + 1, group * OWN), (Z, 1, 4 * KEYS))
+    digits = digits.reshape(Z, 4, KEYS).astype(jnp.int32)
+    keys = digits[:, 0] + digits[:, 1] * 256 + digits[:, 2] * 65536 + digits[:, 3] * 16777216
+    bases = base_values(keys, jnp.arange(Z, dtype=jnp.int32), y)
+    others = (z + jnp.arange(1, Z, dtype=jnp.int32)) % Z
+    partial = partial_drive(others, row_terms, bases, vectors, (partial,))
 
     pieces = []
     for shift in range(Y):

time: 247 us -> 237 us (0.960)
  blocking collectives: 77.8 us -> 63.8 us
    all_gather x2 -> x1, blocking collectives: 31.2 us -> 17.2 us  [per_device(): near = lax.all_gather(own, ('x', 'core'), axis=1, tiled=True)]
    pallas_call x1 -> x2, Pallas kernels: 95.8 us -> 96.1 us  [partial_drive(): pl.pallas_call(functools.partial(drive_kernel, segments=segments), grid=(...]
  transfers between devices with their start and end apart: 4 -> 4, of which waited for: 4 -> 4; matrix products, arithmetic and copies ran while one was open for 0% -> 0% of each run, Pallas kernels for 0% -> 5%
where the time goes in v2:
time: 237 us
  Pallas kernels  108 us (46%)
  blocking collectives  63.8 us (27%)
  waiting for transfers between devices  37.8 us (16%)
  between operations  14.2 us (6%)
  local copies, waits for them, and re-layouts  6.55 us (3%)
  starting transfers between devices  3.66 us (2%)
  other arithmetic  3.22 us (1%)
    pallas_call x2, Pallas kernels, partial_drive(): pl.pallas_call(functools.partial(drive_kernel, segments=segments), grid=(...  96.1 us
    all_to_all x4, blocking collectives, spread_to(): lax.all_to_all(jnp.broadcast_to(value, (count, *value.shape)), axes, 0, 0)  46.6 us
    all_gather x1, waiting for transfers between devices, per_device(): vectors = lax.all_gather(near, 'z')  31.5 us
    all_gather x1, blocking collectives, per_device(): near = lax.all_gather(own, ('x', 'core'), axis=1, tiled=True)  17.2 us
    ppermute x3, waiting for transfers between devices, per_device(): piece = lax.ppermute(piece, 'y', [(i, (i + shift) % Y) for i in range(Y)])  6.31 us
    pallas_call x1, Pallas kernels, per_device(): pl.pallas_call(second_kernel, out_shape=(jax.ShapeDtypeStruct((VECS, OWN)...  4.84 us
  transfers between devices with their start and end apart: 4, of which 4 were waited for; matrix products, arithmetic and copies ran while one was open for 0% of the time, Pallas kernels for 5%

profile of v2, /device:TPU:1, one launch (start us, length us, event | category | flops | bytes accessed | tf_op | source)
XLA Modules:
  0.0 236.7 jit_solution(1373913276607607732)
XLA Ops:
  7.2 0.7 reshape.110
  7.9 0.7 and_convert_fusion
  8.7 0.8 maximum_maximum_fusion
  9.6 17.2 %all_gather.9 = bf16[48,4096]{1,0:T(8,128)(2,1)} all-gather(bf16[48,512]{1,0:T(8,128)(2,1)S(1)} %maximum_maximum_fusion), channel_id=1, replica_groups=mesh['x'=4,'core'=2,'z'=8,'y'=4] {'x','core'}, dimensions={1}, use_global_device_ids=true | all-gather | bytes 442368 | tf_op jit(solution)/shard_map/all_gather | solution.py:175
  26.8 0.7 broadcast_in_dim.44
  27.8 1.0 copy-done
  28.8 12.0 %shard_map.66.refs_0_ = f32[48,2048]{1,0:T(8,128)S(1)} custom-call(s32[1]{0:T(128)} %constant.106.clone.1.places_ref, s32[1,2048]{1,0:T(1,128)S(1)} %add_multiply_fusion.rows_ref, s32[128,128]{1,0:T(8,128)S(1)} %broadcast_in_dim.46.bases_ref, bf16[1,48,4096]{2,1,0:T(8,128)(2,1)S(1)} %bitcast.21), custom_call_target="tpu_custom_call" | custom-call | flops 12582912000 | bytes 393216 | tf_op jit(solution)/shard_map/pallas_call | solution.py:68
  40.8 31.5 %all-gather.3.cloned.1.call-done = bf16[384,4096]{1,0:T(8,128)(2,1)} async-done(((bf16[48,4096]{1,0:T(8,128)(2,1)}), bf16[384,4096]{1,0:T(8,128)(2,1)}) %all-gather.3.cloned.1.call-update) | async-done | bytes 3145744 | tf_op jit(solution)/shard_map/all_gather | solution.py:176
  72.3 0.8 convert_reduce_fusion
  73.7 1.9 copy-done.1
  75.6 84.2 %shard_map.67 = f32[48,2048]{1,0:T(8,128)S(1)} custom-call(s32[7]{0:T(128)S(1)} %and_select_fusion.places_ref, s32[1,2048]{1,0:T(1,128)S(1)} %add_multiply_fusion.rows_ref, s32[1024,128]{1,0:T(8,128)S(1)} %broadcast_in_dim.43.bases_ref, bf16[8,48,4096]{2,1,0:T(8,128)(2,1)S(1)} %bitcast.23, f32[48,2048]{1,0:T(8,128)S(1)} %shard_map.66.refs_0_), custom_call_target="tpu_custom_call" | custom-call | flops 88080384000 | bytes 3145728 | tf_op jit(solution)/shard_map/pallas_call | solution.py:68
  159.8 2.5 %collective-permute-start.2 = (f32[48,512]{1,0:T(8,128)S(1)}, f32[48,512]{1,0:T(8,128)S(1)}, u32[]{:S(2)}, u32[]{:S(2)}) collective-permute-start(f32[48,512]{1,0:T(8,128)S(1)} %get-tuple-element.21), channel_id=1, source_target_pairs={{0,3},{1,0},{2,1},{3,2},{4,7},{5,4},{6,5},{7,6},{8,11},{9,8},{10,9... | collective-permute-start | bytes 294920 | tf_op jit(solution)/shard_map/ppermute | solution.py:193
  163.9 3.4 %collective-permute-done.1 = f32[48,512]{1,0:T(8,128)S(1)} collective-permute-done((f32[48,512]{1,0:T(8,128)S(1)}, f32[48,512]{1,0:T(8,128)S(1)}, u32[]{:S(2)}, u32[]{:S(2)}) %collective-permute-start.1) | collective-permute-done | bytes 98336 | tf_op jit(solution)/shard_map/ppermute | solution.py:193
  167.3 2.4 %collective-permute-done = f32[48,512]{1,0:T(8,128)S(1)} collective-permute-done((f32[48,512]{1,0:T(8,128)S(1)}, f32[48,512]{1,0:T(8,128)S(1)}, u32[]{:S(2)}, u32[]{:S(2)}) %collective-permute-start) | collective-permute-done | bytes 98336 | tf_op jit(solution)/shard_map/ppermute | solution.py:193
  169.7 0.8 pad_maximum_fusion.pieces_ref
  170.5 1.9 shard_map.68
  172.4 0.7 broadcast_in_dim.47
  173.0 10.2 %all_to_all.20 = f32[8,8,128]{2,1,0:T(8,128)S(1)} all-to-all(f32[8,8,128]{2,1,0:T(8,128)S(1)} %broadcast_in_dim.47), channel_id=1, replica_groups=mesh['x'=4,'core'=2,'z'=8,'y'=4] {'x','core'}, dimensions={0} | all-to-all | bytes 65536 | tf_op jit(solution)/shard_map/all_to_all | solution.py:152
  183.2 14.1 %all_to_all.21.grams_ref = f32[32,8,128]{2,1,0:T(8,128)} all-to-all(f32[32,8,128]{2,1,0:T(8,128)S(1)} %broadcast_in_dim.48), channel_id=1, replica_groups=mesh['x'=4,'core'=2,'z'=8,'y'=4] {'z','y'}, dimensions={0} | all-to-all | bytes 262144 | tf_op jit(solution)/shard_map/all_to_all | solution.py:152
  197.3 4.8 %shard_map.69 = (f32[32,512]{1,0:T(8,128)}, f32[8,128]{1,0:T(8,128)}, f32[32,32]{1,0:T(8,128)}) custom-call(f32[32,8,128]{2,1,0:T(8,128)} %all_to_all.21.grams_ref, f32[32,512]{1,0:T(8,128)} %get-tuple-element.13.grown_ref), custom_call_target="tpu_custom_call" | custom-call | tf_op jit(solution)/shard_map/pallas_call | solution.py:204
  202.2 0.7 broadcast_in_dim.49
  202.9 9.2 %all_to_all.22 = f32[8,8,128]{2,1,0:T(8,128)S(1)} all-to-all(f32[8,8,128]{2,1,0:T(8,128)S(1)} %broadcast_in_dim.49), channel_id=1, replica_groups=mesh['x'=4,'core'=2,'z'=8,'y'=4] {'x','core'}, dimensions={0} | all-to-all | bytes 65536 | tf_op jit(solution)/shard_map/all_to_all | solution.py:152
  212.1 13.1 %all_to_all.23.grams_ref = f32[32,8,128]{2,1,0:T(8,128)} all-to-all(f32[32,8,128]{2,1,0:T(8,128)S(1)} %broadcast_in_dim.50), channel_id=1, replica_groups=mesh['x'=4,'core'=2,'z'=8,'y'=4] {'z','y'}, dimensions={0} | all-to-all | bytes 262144 | tf_op jit(solution)/shard_map/all_to_all | solution.py:152
  225.2 4.6 %shard_map.70 = (f32[32,512]{1,0:T(8,128)}, f32[32,32]{1,0:T(8,128)}) custom-call(f32[32,8,128]{2,1,0:T(8,128)} %all_to_all.23.grams_ref, f32[32,512]{1,0:T(8,128)} %get-tuple-element.15.first_ref, f32[32,32]{1,0:T(8,128)} %get-tuple-element.11.upper_ref), custom_call_target="tpu_custom_call" | custom-call | tf_op jit(solution)/shard_map/pallas_call | solution.py:212
  (31 shorter events, 2.7 us)
Async XLA Ops:
  7.2 65.1 %all-gather.3.cloned.1.call-start = ((), (), s32[]{:S(2)}) async-start(), calls=%async_computation.4 | async-start | bytes 3538944 | tf_op jit(solution)/shard_map/all_gather | solution.py:176
  27.8 1.0 copy-start
  73.7 1.9 copy-start.1
  159.8 4.1 %collective-permute-start.2 = (f32[48,512]{1,0:T(8,128)S(1)}, f32[48,512]{1,0:T(8,128)S(1)}, u32[]{:S(2)}, u32[]{:S(2)}) collective-permute-start(f32[48,512]{1,0:T(8,128)S(1)} %get-tuple-element.21), channel_id=1, source_target_pairs={{0,3},{1,0},{2,1},{3,2},{4,7},{5,4},{6,5},{7,6},{8,11},{9,8},{10,9... | collective-permute-start | bytes 294920 | tf_op jit(solution)/shard_map/ppermute | solution.py:193
  162.3 5.1 %collective-permute-start.1 = (f32[48,512]{1,0:T(8,128)S(1)}, f32[48,512]{1,0:T(8,128)S(1)}, u32[]{:S(2)}, u32[]{:S(2)}) collective-permute-start(f32[48,512]{1,0:T(8,128)S(1)} %get-tuple-element.22), channel_id=1, source_target_pairs={{0,2},{1,3},{2,0},{3,1},{4,6},{5,7},{6,4},{7,5},{8,10},{9,11},{10,... | collective-permute-start | bytes 294920 | tf_op jit(solution)/shard_map/ppermute | solution.py:193
  162.8 6.9 %collective-permute-start = (f32[48,512]{1,0:T(8,128)S(1)}, f32[48,512]{1,0:T(8,128)S(1)}, u32[]{:S(2)}, u32[]{:S(2)}) collective-permute-start(f32[48,512]{1,0:T(8,128)S(1)} %get-tuple-element.23), channel_id=1, source_target_pairs={{0,1},{1,2},{2,3},{3,0},{4,5},{5,6},{6,7},{7,4},{8,9},{9,10},{10,1... | collective-permute-start | bytes 294920 | tf_op jit(solution)/shard_map/ppermute | solution.py:193
Sparse Core Ops, SparseCore 0:
  26.9 45.3 all-gather.2

commit v3 on v2

--- a/solution.py
+++ b/solution.py
@@ -18,6 +18,7 @@
 ROWS = OWN * Y
 SEG = OWN * X * CORE
 GROUP = 32
+GRAM_ROW = 40
 LANES = 512
 KEYS = SEG // KEYCOLS
 SCALE = 2.0 / math.sqrt(5461.25 * N)
@@ -39,7 +40,7 @@
 
 
 def drive_kernel(places_ref, rows_ref, bases_ref, vectors_ref, *refs, segments):
-    out_ref = refs[-1]
+    out_ref = refs[len(refs) // 2]
     spread = lax.broadcasted_iota(jnp.int32, (GROUP, 128), 0) * jnp.int32(668265261)
     starts = [rows_ref[:, 128 * k : 128 * k + 128] + spread for k in range(LANES // 128)]
     groups = SEG // GROUP
@@ -59,6 +60,20 @@
 
     initial = refs[0][...] if len(refs) > 1 else jnp.zeros(out_ref.shape, jnp.float32)
     out_ref[...] = lax.fori_loop(0, segments, body, initial)
+    if len(refs) > 1:
+        gram_ref = refs[2]
+
+        @pl.when(pl.program_id(0) == 0)
+        def _():
+            total = jnp.zeros((VECS, VECS), jnp.float32)
+            for place in range(Z):
+                own = vectors_ref[place][:VECS]
+                total += lax.dot_general(
+                    own, own, (((1,), (1,)), ((), ())), preferred_element_type=jnp.float32
+                )
+            gram_ref[...] = pack_gram(total / N)
+
+        out_ref[GRAM_ROW:, :128] = gram_ref[...]
 
 
 def partial_drive(places, row_terms, bases, vectors, earlier=()):
@@ -77,6 +92,7 @@
         + [lanes] * len(earlier),
         out_specs=lanes,
         out_shape=jax.ShapeDtypeStruct((PAD, ROWS), jnp.float32),
+        scratch_shapes=[pltpu.VMEM((8, 128), jnp.float32)] * len(earlier),
         cost_estimate=pl.CostEstimate(
             flops=hashes * 1500, bytes_accessed=vectors.size * 2, transcendentals=0
         ),
@@ -104,15 +120,24 @@
     ) / N
 
 
-def factor(gram):
+def dot(left, right):
+    return jnp.dot(left, right, precision=HIGH, preferred_element_type=jnp.float32)
+
+
+def factor(gram, floor=0.0):
     rows = lax.broadcasted_iota(jnp.int32, (VECS, VECS), 0)
     columns = lax.broadcasted_iota(jnp.int32, (VECS, VECS), 1)
     work = jnp.concatenate((gram, (rows == columns).astype(jnp.float32)), axis=1)
     row_at = lax.broadcasted_iota(jnp.int32, (VECS, 1), 0)
+    column_at = lax.broadcasted_iota(jnp.int32, (1, 2 * VECS), 1)
     scales = jnp.zeros((VECS, 1), jnp.float32)
     for j in range(VECS):
         pivot_row = work[j : j + 1, :]
         pivot = work[j : j + 1, j : j + 1]
+        if floor:
+            pivot = jnp.maximum(pivot, jnp.maximum(floor * gram[j : j + 1, j : j + 1], 1e-30))
+            pivot_row = jnp.where(column_at == j, pivot, pivot_row)
+            work = jnp.where(row_at == j, pivot_row, work)
         ratio = jnp.where(row_at > j, work[:, j : j + 1] / pivot, 0.0)
         scales = jnp.where(row_at == j, lax.rsqrt(pivot), scales)
         work = work - ratio * pivot_row
@@ -121,31 +146,37 @@
     return upper, work[:, VECS:]
 
 
-def first_kernel(pieces_ref, state_ref, grown_ref, gram_ref):
+def first_kernel(order_ref, pieces_ref, state_ref, scaled_ref, gram_ref, upper_ref):
     drive = pieces_ref[0] + pieces_ref[1] + pieces_ref[2] + pieces_ref[3]
     state = jnp.tanh(SCALE * drive[VECS : VECS + 1])
     grown = (SCALE * (1.0 - state * state)) * drive[:VECS]
+    inputs = pieces_ref[order_ref[0]][GRAM_ROW:, :128]
+    for k in range(1, Y):
+        inputs += pieces_ref[order_ref[k]][GRAM_ROW:, :128]
+    upper, inverse = factor(unpack_gram(inputs), 1e-6)
+    scaled = dot(inverse, grown)
     state_ref[...] = state
-    grown_ref[...] = grown
-    gram_ref[...] = pack_gram(gram_of(grown))
-
-
-def second_kernel(grams_ref, grown_ref, first_ref, gram_ref, upper_ref):
-    upper, inverse = factor(unpack_gram(jnp.sum(grams_ref[...], axis=0)))
-    first = jnp.dot(inverse, grown_ref[...], precision=HIGH, preferred_element_type=jnp.float32)
-    first_ref[...] = first
+    scaled_ref[...] = scaled
+    gram_ref[...] = pack_gram(gram_of(scaled))
     upper_ref[...] = upper
-    gram_ref[...] = pack_gram(gram_of(first))
-
-
-def third_kernel(grams_ref, first_ref, upper_ref, result_ref, product_ref):
-    upper, inverse = factor(unpack_gram(jnp.sum(grams_ref[...], axis=0)))
-    result_ref[...] = jnp.dot(
-        inverse, first_ref[...], precision=HIGH, preferred_element_type=jnp.float32
-    )
-    product_ref[...] = jnp.dot(
-        upper, upper_ref[...], precision=HIGH, preferred_element_type=jnp.float32
-    )
+
+
+def second_kernel(grams_ref, scaled_ref, input_upper_ref, result_ref, product_ref, upper_ref):
+    gram = unpack_gram(jnp.sum(grams_ref[...], axis=0))
+    near_upper, inverse = factor(gram)
+    first = dot(inverse, scaled_ref[...])
+    upper = dot(near_upper, input_upper_ref[...])
+    gram_two = lax.dot_general(
+        dot(inverse, gram),
+        inverse,
+        (((1,), (1,)), ((), ())),
+        precision=HIGH,
+        preferred_element_type=jnp.float32,
+    )
+    second_upper, second_inverse = factor(gram_two)
+    result_ref[...] = dot(second_inverse, first)
+    product_ref[...] = dot(second_upper, upper)
+    upper_ref[...] = upper
 
 
 def spread_to(value, axes, count):
@@ -193,29 +224,23 @@
             piece = lax.ppermute(piece, "y", [(i, (i + shift) % Y) for i in range(Y)])
         pieces.append(piece)
 
-    state, grown, gram = pl.pallas_call(
+    order = (y - jnp.arange(Y, dtype=jnp.int32)) % Y
+    vmem = pl.BlockSpec(memory_space=pltpu.VMEM)
+    square = jax.ShapeDtypeStruct((VECS, VECS), jnp.float32)
+    wide = jax.ShapeDtypeStruct((VECS, OWN), jnp.float32)
+    state, scaled, gram, input_upper = pl.pallas_call(
         first_kernel,
+        in_specs=[pl.BlockSpec(memory_space=pltpu.SMEM), vmem],
         out_shape=(
             jax.ShapeDtypeStruct((1, OWN), jnp.float32),
-            jax.ShapeDtypeStruct((VECS, OWN), jnp.float32),
+            wide,
             jax.ShapeDtypeStruct((8, 128), jnp.float32),
+            square,
         ),
-    )(jnp.stack(pieces))
-    first, gram, upper = pl.pallas_call(
-        second_kernel,
-        out_shape=(
-            jax.ShapeDtypeStruct((VECS, OWN), jnp.float32),
-            jax.ShapeDtypeStruct((8, 128), jnp.float32),
-            jax.ShapeDtypeStruct((VECS, VECS), jnp.float32),
-        ),
-    )(gather_grams(gram), grown)
-    result, product = pl.pallas_call(
-        third_kernel,
-        out_shape=(
-            jax.ShapeDtypeStruct((VECS, OWN), jnp.float32),
-            jax.ShapeDtypeStruct((VECS, VECS), jnp.float32),
-        ),
-    )(gather_grams(gram), first, upper)
+    )(order, jnp.stack(pieces))
+    result, product, upper = pl.pallas_call(second_kernel, out_shape=(wide, square, square))(
+        gather_grams(gram), scaled, input_upper
+    )
     return result, state.reshape(OWN), product, upper
 
 

time: 237 us -> 218 us (0.920)
  blocking collectives: 63.8 us -> 41.4 us
  Pallas kernels: 108 us -> 111 us
    all_to_all x4 -> x2, blocking collectives: 46.6 us -> 24.3 us  [spread_to(): lax.all_to_all(jnp.broadcast_to(value, (count, *value.shape)), axes, 0, 0)]
    pallas_call x3 -> x2, Pallas kernels: 11.4 us -> 14.4 us  [the longest x1 7.85 us: per_device(): pl.pallas_call(second_kernel, out_shape=(wide, square, square))]
  transfers between devices with their start and end apart: 4 -> 4, of which waited for: 4 -> 3; matrix products, arithmetic and copies ran while one was open for 0% -> 1% of each run, Pallas kernels for 5% -> 6%
where the time goes in v3:
time: 218 us
  Pallas kernels  111 us (51%)
  blocking collectives  41.4 us (19%)
  waiting for transfers between devices  37.3 us (17%)
  between operations  14.2 us (7%)
  local copies, waits for them, and re-layouts  5.85 us (3%)
  other arithmetic  3.73 us (2%)
  starting transfers between devices  3.67 us (2%)
    pallas_call x2, Pallas kernels, partial_drive(): pl.pallas_call(functools.partial(drive_kernel, segments=segments), grid=(...  96.9 us
    all_gather x1, waiting for transfers between devices, per_device(): vectors = lax.all_gather(near, 'z')  31.5 us
    all_to_all x2, blocking collectives, spread_to(): lax.all_to_all(jnp.broadcast_to(value, (count, *value.shape)), axes, 0, 0)  24.3 us
    all_gather x1, blocking collectives, per_device(): near = lax.all_gather(own, ('x', 'core'), axis=1, tiled=True)  17.2 us
    pallas_call x1, Pallas kernels, per_device(): pl.pallas_call(second_kernel, out_shape=(wide, square, square))  7.85 us
    pallas_call x1, Pallas kernels, per_device(): pl.pallas_call(first_kernel, in_specs=[pl.BlockSpec(memory_space=pltpu.SM...  6.6 us
    ppermute x3, waiting for transfers between devices, per_device(): piece = lax.ppermute(piece, 'y', [(i, (i + shift) % Y) for i in range(Y)])  5.79 us
  transfers between devices with their start and end apart: 4, of which 3 were waited for; matrix products, arithmetic and copies ran while one was open for 1% of the time, Pallas kernels for 6%

profile of v3, /device:TPU:1, one launch (start us, length us, event | category | flops | bytes accessed | tf_op | source)
XLA Modules:
  0.0 217.5 jit_solution(903469829736282771)
XLA Ops:
  7.2 0.7 reshape.110
  7.9 0.7 and_convert_fusion
  8.7 0.8 maximum_maximum_fusion
  9.6 17.2 %all_gather.9 = bf16[48,4096]{1,0:T(8,128)(2,1)} all-gather(bf16[48,512]{1,0:T(8,128)(2,1)S(1)} %maximum_maximum_fusion), channel_id=1, replica_groups=mesh['x'=4,'core'=2,'z'=8,'y'=4] {'x','core'}, dimensions={1}, use_global_device_ids=true | all-gather | bytes 442368 | tf_op jit(solution)/shard_map/all_gather | solution.py:206
  26.8 0.7 broadcast_in_dim.38
  27.8 1.0 copy-done
  28.8 12.0 %shard_map.66.refs_0_ = f32[48,2048]{1,0:T(8,128)S(1)} custom-call(s32[1]{0:T(128)} %constant.115.clone.1.places_ref, s32[1,2048]{1,0:T(1,128)S(1)} %add_multiply_fusion.rows_ref, s32[128,128]{1,0:T(8,128)S(1)} %broadcast_in_dim.40.bases_ref, bf16[1,48,4096]{2,1,0:T(8,128)(2,1)S(1)} %bitcast.21), custom_call_target="tpu_custom_call" | custom-call | flops 12582912000 | bytes 393216 | tf_op jit(solution)/shard_map/pallas_call | solution.py:83
  40.8 31.5 %all-gather.3.cloned.1.call-done = bf16[384,4096]{1,0:T(8,128)(2,1)} async-done(((bf16[48,4096]{1,0:T(8,128)(2,1)}), bf16[384,4096]{1,0:T(8,128)(2,1)}) %all-gather.3.cloned.1.call-update) | async-done | bytes 3145744 | tf_op jit(solution)/shard_map/all_gather | solution.py:207
  72.3 0.8 convert_reduce_fusion
  73.5 0.2 broadcast_in_dim.37.bases_ref
  73.7 1.9 copy-done.1
  75.6 84.9 %shard_map.67 = f32[48,2048]{1,0:T(8,128)S(1)} custom-call(s32[7]{0:T(128)S(1)} %and_select_fusion.places_ref, s32[1,2048]{1,0:T(1,128)S(1)} %add_multiply_fusion.rows_ref, s32[1024,128]{1,0:T(8,128)S(1)} %broadcast_in_dim.37.bases_ref, bf16[8,48,4096]{2,1,0:T(8,128)(2,1)S(1)} %bitcast.23, f32[48,2048]{1,0:T(8,128)S(1)} %shard_map.66.refs_0_), custom_call_target="tpu_custom_call" | custom-call | flops 88080384000 | bytes 3145728 | tf_op jit(solution)/shard_map/pallas_call | solution.py:83
  160.5 2.5 %collective-permute-start.2 = (f32[48,512]{1,0:T(8,128)S(1)}, f32[48,512]{1,0:T(8,128)S(1)}, u32[]{:S(2)}, u32[]{:S(2)}) collective-permute-start(f32[48,512]{1,0:T(8,128)S(1)} %get-tuple-element.19), channel_id=1, source_target_pairs={{0,3},{1,0},{2,1},{3,2},{4,7},{5,4},{6,5},{7,6},{8,11},{9,8},{10,9... | collective-permute-start | bytes 294920 | tf_op jit(solution)/shard_map/ppermute | solution.py:224
  163.0 0.6 collective-permute-start.1
  163.6 0.6 collective-permute-start
  164.2 0.5 and_select_fusion.1.order_ref
  164.7 3.4 %collective-permute-done.1 = f32[48,512]{1,0:T(8,128)S(1)} collective-permute-done((f32[48,512]{1,0:T(8,128)S(1)}, f32[48,512]{1,0:T(8,128)S(1)}, u32[]{:S(2)}, u32[]{:S(2)}) %collective-permute-start.1) | collective-permute-done | bytes 98336 | tf_op jit(solution)/shard_map/ppermute | solution.py:224
  168.1 2.4 %collective-permute-done = f32[48,512]{1,0:T(8,128)S(1)} collective-permute-done((f32[48,512]{1,0:T(8,128)S(1)}, f32[48,512]{1,0:T(8,128)S(1)}, u32[]{:S(2)}, u32[]{:S(2)}) %collective-permute-start) | collective-permute-done | bytes 98336 | tf_op jit(solution)/shard_map/ppermute | solution.py:224
  170.5 0.8 pad_maximum_fusion.pieces_ref
  171.3 6.6 %shard_map.68 = (f32[1,512]{1,0:T(1,128)}, f32[32,512]{1,0:T(8,128)}, f32[8,128]{1,0:T(8,128)}, f32[32,32]{1,0:T(8,128)}) custom-call(s32[4]{0:T(128)} %and_select_fusion.1.order_ref, f32[4,48,512]{2,1,0:T(8,128)} %pad_maximum_fusion.pieces_ref), custom_call_target="tpu_custom_call" | custom-call | tf_op jit(solution)/shard_map/pallas_call | solution.py:231
  177.9 0.7 broadcast_in_dim.41
  178.5 10.2 %all_to_all.10 = f32[8,8,128]{2,1,0:T(8,128)S(1)} all-to-all(f32[8,8,128]{2,1,0:T(8,128)S(1)} %broadcast_in_dim.41), channel_id=1, replica_groups=mesh['x'=4,'core'=2,'z'=8,'y'=4] {'x','core'}, dimensions={0} | all-to-all | bytes 65536 | tf_op jit(solution)/shard_map/all_to_all | solution.py:183
  188.7 14.1 %all_to_all.11.grams_ref = f32[32,8,128]{2,1,0:T(8,128)} all-to-all(f32[32,8,128]{2,1,0:T(8,128)S(1)} %broadcast_in_dim.42), channel_id=1, replica_groups=mesh['x'=4,'core'=2,'z'=8,'y'=4] {'z','y'}, dimensions={0} | all-to-all | bytes 262144 | tf_op jit(solution)/shard_map/all_to_all | solution.py:183
  202.8 7.8 %shard_map.69 = (f32[32,512]{1,0:T(8,128)}, f32[32,32]{1,0:T(8,128)}, f32[32,32]{1,0:T(8,128)}) custom-call(f32[32,8,128]{2,1,0:T(8,128)} %all_to_all.11.grams_ref, f32[32,512]{1,0:T(8,128)} %get-tuple-element.12.scaled_ref, f32[32,32]{1,0:T(8,128)} %get-tuple-element.13.input_upper_ref), custom_call_target="tpu_custom_call" | custom-call | tf_op jit(solution)/shard_map/pallas_call | solution.py:241
  (26 shorter events, 0.9 us)
Async XLA Ops:
  7.2 65.1 %all-gather.3.cloned.1.call-start = ((), (), s32[]{:S(2)}) async-start(), calls=%async_computation.2 | async-start | bytes 3538944 | tf_op jit(solution)/shard_map/all_gather | solution.py:207
  27.8 1.0 copy-start
  73.7 1.9 copy-start.1
  160.5 4.2 %collective-permute-start.2 = (f32[48,512]{1,0:T(8,128)S(1)}, f32[48,512]{1,0:T(8,128)S(1)}, u32[]{:S(2)}, u32[]{:S(2)}) collective-permute-start(f32[48,512]{1,0:T(8,128)S(1)} %get-tuple-element.19), channel_id=1, source_target_pairs={{0,3},{1,0},{2,1},{3,2},{4,7},{5,4},{6,5},{7,6},{8,11},{9,8},{10,9... | collective-permute-start | bytes 294920 | tf_op jit(solution)/shard_map/ppermute | solution.py:224
  163.0 5.1 %collective-permute-start.1 = (f32[48,512]{1,0:T(8,128)S(1)}, f32[48,512]{1,0:T(8,128)S(1)}, u32[]{:S(2)}, u32[]{:S(2)}) collective-permute-start(f32[48,512]{1,0:T(8,128)S(1)} %get-tuple-element.20), channel_id=1, source_target_pairs={{0,2},{1,3},{2,0},{3,1},{4,6},{5,7},{6,4},{7,5},{8,10},{9,11},{10,... | collective-permute-start | bytes 294920 | tf_op jit(solution)/shard_map/ppermute | solution.py:224
  163.6 6.9 %collective-permute-start = (f32[48,512]{1,0:T(8,128)S(1)}, f32[48,512]{1,0:T(8,128)S(1)}, u32[]{:S(2)}, u32[]{:S(2)}) collective-permute-start(f32[48,512]{1,0:T(8,128)S(1)} %get-tuple-element.21), channel_id=1, source_target_pairs={{0,1},{1,2},{2,3},{3,0},{4,5},{5,6},{6,7},{7,4},{8,9},{9,10},{10,1... | collective-permute-start | bytes 294920 | tf_op jit(solution)/shard_map/ppermute | solution.py:224
Sparse Core Ops, SparseCore 0:
  26.9 45.3 all-gather.2

commit v4 on v3

--- a/solution.py
+++ b/solution.py
@@ -18,9 +18,11 @@
 ROWS = OWN * Y
 SEG = OWN * X * CORE
 GROUP = 32
+SPARE = 40
 GRAM_ROW = 40
 LANES = 512
 KEYS = SEG // KEYCOLS
+GRAM_TILE = 4 * (KEYS // 8)
 SCALE = 2.0 / math.sqrt(5461.25 * N)
 HIGH = lax.Precision.HIGHEST
 VMEM_LIMIT = 48 * 2**20
@@ -39,71 +41,109 @@
     return (value.astype(jnp.int8) ^ jnp.int8(-128)).astype(jnp.bfloat16)
 
 
-def drive_kernel(places_ref, rows_ref, bases_ref, vectors_ref, *refs, segments):
-    out_ref = refs[len(refs) // 2]
+def spare_tile(block_ref, tile):
+    return block_ref[SPARE - 8 : SPARE + 8, 128 * tile : 128 * tile + 128].astype(jnp.float32)[8:]
+
+
+def block_kernel(near_ref, digits_ref, block_ref):
+    block_ref[...] = near_ref[...]
+    own = near_ref[:VECS, :]
+    gram = lax.dot_general(own, own, (((1,), (1,)), ((), ())), preferred_element_type=jnp.float32)
+    rest = pack_gram(gram / N)
+    tiles = [digits_ref[:, 128 * k : 128 * k + 128] for k in range(GRAM_TILE)]
+    for _ in range(3):
+        part = rest.astype(jnp.bfloat16).astype(jnp.float32)
+        tiles.append(part)
+        rest = rest - part
+    for k, tile in enumerate(tiles):
+        lanes = slice(128 * k, 128 * k + 128)
+        above = near_ref[SPARE - 8 : SPARE + 8, lanes].astype(jnp.float32)[:8]
+        block_ref[SPARE - 8 : SPARE + 8, lanes] = jnp.concatenate((above, tile)).astype(jnp.bfloat16)
+
+
+def drive_kernel(places_ref, rows_ref, *refs, blocks, earlier):
+    block_refs = refs[:blocks]
+    earlier_refs = refs[blocks : blocks + 2 * earlier]
+    out_ref, grams_ref, vectors_ref, bases_ref = refs[blocks + 2 * earlier :]
+    groups = SEG // GROUP
+
+    @pl.when(pl.program_id(0) == 0)
+    def _():
+        for slot in range(Z):
+            if earlier:
+                grams_ref[slot] = earlier_refs[1][slot]
+            else:
+                grams_ref[slot] = jnp.zeros((8, 128), jnp.float32)
+        steps = lax.broadcasted_iota(jnp.int32, (8, 128), 0) * jnp.int32(GROUP)
+        for k in range(blocks):
+            place = places_ref[k]
+            vectors_ref[k] = block_refs[k][...]
+            gram = jnp.zeros((8, 128), jnp.float32)
+            for part in range(3):
+                gram = gram + spare_tile(block_refs[k], GRAM_TILE + part)
+            grams_ref[place] = gram
+            first_column = (place * Y + places_ref[Z]) * SEG
+            for part in range(KEYS // 8):
+                keys = jnp.zeros((8, 128), jnp.int32)
+                for digit in range(4):
+                    tile = spare_tile(block_refs[k], digit * (KEYS // 8) + part)
+                    keys = keys + tile.astype(jnp.int32) * jnp.int32(256**digit)
+                for row in range(8):
+                    key = part * 8 + row
+                    columns = first_column + key * KEYCOLS + steps
+                    at = k * groups + key * 8
+                    bases_ref[at : at + 8, :] = keys[row : row + 1] + columns * jnp.int32(668265261)
+
     spread = lax.broadcasted_iota(jnp.int32, (GROUP, 128), 0) * jnp.int32(668265261)
     starts = [rows_ref[:, 128 * k : 128 * k + 128] + spread for k in range(LANES // 128)]
-    groups = SEG // GROUP
 
     def body(number, total):
-        place = places_ref[number]
-        first = pl.multiple_of(place * groups, groups)
+        first = pl.multiple_of(number * groups, groups)
         parts = []
         for group in range(groups):
             base = bases_ref[pl.ds(first + group, 1), :]
             parts.append(jnp.concatenate([coupling(base + start) for start in starts], axis=1))
         return total + jnp.dot(
-            vectors_ref[place],
+            vectors_ref[number],
             jnp.concatenate(parts, axis=0),
             preferred_element_type=jnp.float32,
         )
 
-    initial = refs[0][...] if len(refs) > 1 else jnp.zeros(out_ref.shape, jnp.float32)
-    out_ref[...] = lax.fori_loop(0, segments, body, initial)
-    if len(refs) > 1:
-        gram_ref = refs[2]
-
-        @pl.when(pl.program_id(0) == 0)
-        def _():
-            total = jnp.zeros((VECS, VECS), jnp.float32)
-            for place in range(Z):
-                own = vectors_ref[place][:VECS]
-                total += lax.dot_general(
-                    own, own, (((1,), (1,)), ((), ())), preferred_element_type=jnp.float32
-                )
-            gram_ref[...] = pack_gram(total / N)
-
-        out_ref[GRAM_ROW:, :128] = gram_ref[...]
-
-
-def partial_drive(places, row_terms, bases, vectors, earlier=()):
-    segments = places.shape[0]
+    initial = earlier_refs[0][...] if earlier else jnp.zeros(out_ref.shape, jnp.float32)
+    out_ref[...] = lax.fori_loop(0, blocks, body, initial)
+    gram = grams_ref[0]
+    for slot in range(1, Z):
+        gram = gram + grams_ref[slot]
+    out_ref[GRAM_ROW:, :128] = gram
+
+
+def partial_drive(places, row_terms, blocks, earlier=()):
     lanes = pl.BlockSpec((PAD, LANES), lambda i: (0, i))
-    hashes = segments * SEG * ROWS
+    grams = pl.BlockSpec((Z, 8, 128), lambda i: (0, 0, 0))
+    count = len(blocks)
     return pl.pallas_call(
-        functools.partial(drive_kernel, segments=segments),
+        functools.partial(drive_kernel, blocks=count, earlier=len(earlier) // 2),
         grid=(ROWS // LANES,),
         in_specs=[
             pl.BlockSpec(memory_space=pltpu.SMEM),
             pl.BlockSpec((1, LANES), lambda i: (0, i)),
-            pl.BlockSpec(bases.shape, lambda i: (0, 0)),
-            pl.BlockSpec(vectors.shape, lambda i: (0, 0, 0)),
         ]
-        + [lanes] * len(earlier),
-        out_specs=lanes,
-        out_shape=jax.ShapeDtypeStruct((PAD, ROWS), jnp.float32),
-        scratch_shapes=[pltpu.VMEM((8, 128), jnp.float32)] * len(earlier),
+        + [pl.BlockSpec((PAD, SEG), lambda i: (0, 0))] * count
+        + [lanes, grams][: len(earlier)],
+        out_specs=(lanes, grams),
+        out_shape=(
+            jax.ShapeDtypeStruct((PAD, ROWS), jnp.float32),
+            jax.ShapeDtypeStruct((Z, 8, 128), jnp.float32),
+        ),
+        scratch_shapes=[
+            pltpu.VMEM((count, PAD, SEG), jnp.bfloat16),
+            pltpu.VMEM((count * SEG // GROUP, 128), jnp.int32),
+        ],
         cost_estimate=pl.CostEstimate(
-            flops=hashes * 1500, bytes_accessed=vectors.size * 2, transcendentals=0
+            flops=count * SEG * ROWS * 1500, bytes_accessed=count * PAD * SEG * 2, transcendentals=0
         ),
         compiler_params=pltpu.CompilerParams(vmem_limit_bytes=VMEM_LIMIT),
-    )(places, row_terms, bases, vectors, *earlier)
-
-
-def base_values(keys, places, y):
-    columns = (places[:, None] * Y + y) * SEG + jnp.arange(0, SEG, GROUP, dtype=jnp.int32)[None, :]
-    values = jnp.repeat(keys, KEYCOLS // GROUP, axis=1) + columns * 668265261
-    return jnp.broadcast_to(values.reshape(-1, 1), (values.size, 128))
+    )(places, row_terms, *blocks, *earlier)
 
 
 def pack_gram(gram):
@@ -191,30 +231,33 @@
 def per_device(tangent, activity, block_keys):
     group = lax.axis_index("x") * CORE + lax.axis_index("core")
     z, y = lax.axis_index("z"), lax.axis_index("y")
-    keys = block_keys[0]
-    digits = [jnp.bitwise_and(shift_right(keys, 8 * k), 255).astype(jnp.bfloat16) for k in range(4)]
-    digits = jnp.concatenate(digits + [jnp.zeros(OWN - 4 * KEYS, jnp.bfloat16)])
     own = jnp.concatenate(
-        (
-            tangent,
-            activity.reshape(1, -1),
-            digits.reshape(1, -1),
-            jnp.zeros((PAD - VECS - 2, OWN), jnp.bfloat16),
-        ),
-        axis=0,
+        (tangent, activity.reshape(1, -1), jnp.zeros((PAD - VECS - 1, OWN), jnp.bfloat16)), axis=0
     )
     near = lax.all_gather(own, ("x", "core"), axis=1, tiled=True)
-    vectors = lax.all_gather(near, "z")
+    keys = block_keys[0].reshape(KEYS // 8, 8).T
+    digits = [jnp.bitwise_and(shift_right(keys, 8 * k), 255) for k in range(4)]
+    digits = jnp.repeat(jnp.concatenate(digits, axis=1).astype(jnp.float32), 128, axis=1)
+    near = pl.pallas_call(
+        block_kernel, out_shape=jax.ShapeDtypeStruct((PAD, SEG), jnp.bfloat16)
+    )(near, digits)
     row_ids = group * (N // (X * CORE)) + z * ROWS + jnp.arange(ROWS, dtype=jnp.int32)
     row_terms = (row_ids * 374761393).reshape(1, ROWS)
-    here = base_values(keys[None], z[None], y)
-    partial = partial_drive(jnp.zeros(1, jnp.int32), row_terms, here, near[None])
-    digits = lax.dynamic_slice(vectors, (0, VECS + 1, group * OWN), (Z, 1, 4 * KEYS))
-    digits = digits.reshape(Z, 4, KEYS).astype(jnp.int32)
-    keys = digits[:, 0] + digits[:, 1] * 256 + digits[:, 2] * 65536 + digits[:, 3] * 16777216
-    bases = base_values(keys, jnp.arange(Z, dtype=jnp.int32), y)
-    others = (z + jnp.arange(1, Z, dtype=jnp.int32)) % Z
-    partial = partial_drive(others, row_terms, bases, vectors, (partial,))
+
+    def places(shifts):
+        shifts = jnp.array(shifts + [0] * (Z - len(shifts)), jnp.int32)
+        return jnp.append((z + shifts) % Z, y)
+
+    up = [(i, (i + 1) % Z) for i in range(Z)]
+    down = [(i, (i - 1) % Z) for i in range(Z)]
+    below, above = lax.ppermute(near, "z", up), lax.ppermute(near, "z", down)
+    earlier = partial_drive(places([0]), row_terms, [near])
+    for step in range(1, Z // 2):
+        next_below = lax.ppermute(below, "z", up)
+        next_above = lax.ppermute(above, "z", down) if step + 1 < Z // 2 else None
+        earlier = partial_drive(places([-step, step]), row_terms, [below, above], earlier)
+        below, above = next_below, next_above
+    partial, _ = partial_drive(places([Z // 2]), row_terms, [below], earlier)
 
     pieces = []
     for shift in range(Y):

time: 218 us -> 188 us (0.86)
  waiting for transfers between devices: 37.3 us -> 3.06 us
  between operations: 14.2 us -> 0.81 us
  starting transfers between devices: 3.67 us -> 14.7 us
  Pallas kernels: 111 us -> 116 us
  blocking collectives: 41.4 us -> 45.2 us
    all_gather x1 -> x0, waiting for transfers between devices: 31.5 us -> none  [per_device(): vectors = lax.all_gather(near, 'z')]
    ppermute x0 -> x7, starting transfers between devices: none -> 9.69 us  [the longest x2 5.31 us: per_device(): next_above = lax.ppermute(above, 'z', down) if step + 1 < Z // 2 else None]
    pallas_call x2 -> x6, Pallas kernels: 96.9 us -> 102 us  [the longest x5 99.8 us: partial_drive(): pl.pallas_call(functools.partial(drive_kernel, blocks=count, earlier=len(...]
    all_to_all x2, blocking collectives: 24.3 us -> 28 us  [spread_to(): lax.all_to_all(jnp.broadcast_to(value, (count, *value.shape)), axes, 0, 0)]
    ppermute x3, waiting for transfers between devices: 5.79 us -> 3.05 us  [per_device(): piece = lax.ppermute(piece, 'y', [(i, (i + shift) % Y) for i in range(Y)])]
  transfers between devices with their start and end apart: 4 -> 10, of which waited for: 3 -> 2; matrix products, arithmetic and copies ran while one was open for 1% -> 1% of each run, Pallas kernels for 6% -> 46%
where the time goes in v4:
time: 188 us
  Pallas kernels  116 us (62%)
  blocking collectives  45.2 us (24%)
  starting transfers between devices  14.7 us (8%)
  local copies, waits for them, and re-layouts  5.28 us (3%)
  waiting for transfers between devices  3.06 us (2%)
  other arithmetic  2.42 us (1%)
    pallas_call x5, Pallas kernels, partial_drive(): pl.pallas_call(functools.partial(drive_kernel, blocks=count, earlier=len(...  99.8 us
    all_to_all x2, blocking collectives, spread_to(): lax.all_to_all(jnp.broadcast_to(value, (count, *value.shape)), axes, 0, 0)  28 us
    all_gather x1, blocking collectives, per_device(): near = lax.all_gather(own, ('x', 'core'), axis=1, tiled=True)  17.2 us
    pallas_call x1, Pallas kernels, per_device(): pl.pallas_call(second_kernel, out_shape=(wide, square, square))  7.85 us
    pallas_call x1, Pallas kernels, per_device(): pl.pallas_call(first_kernel, in_specs=[pl.BlockSpec(memory_space=pltpu.SM...  6.6 us
    ppermute x2, starting transfers between devices, per_device(): next_above = lax.ppermute(above, 'z', down) if step + 1 < Z // 2 else None  5.31 us
    ppermute x3, starting transfers between devices, per_device(): piece = lax.ppermute(piece, 'y', [(i, (i + shift) % Y) for i in range(Y)])  5.06 us
    ppermute x2, starting transfers between devices, per_device(): below, above = (lax.ppermute(near, 'z', up), lax.ppermute(near, 'z', down))  4.19 us
  transfers between devices with their start and end apart: 10, of which 2 were waited for; matrix products, arithmetic and copies ran while one was open for 1% of the time, Pallas kernels for 46%

profile of v4, /device:TPU:1, one launch (start us, length us, event | category | flops | bytes accessed | tf_op | source)
XLA Modules:
  0.0 187.7 jit_solution(9558927128303897799)
XLA Ops:
  0.6 0.7 and_reduce_fusion.3
  1.7 0.7 broadcast_bitcast_fusion.digits_ref
  2.5 17.2 %all_gather.3.near_ref = bf16[48,4096]{1,0:T(8,128)(2,1)} all-gather(bf16[48,512]{1,0:T(8,128)(2,1)S(1)} %maximum_maximum_fusion), channel_id=1, replica_groups=mesh['x'=4,'core'=2,'z'=8,'y'=4] {'x','core'}, dimensions={1}, use_global_device_ids=true | all-gather | bytes 442368 | tf_op jit(solution)/shard_map/all_gather | solution.py:237
  19.7 2.0 %shard_map.111.refs_0_ = bf16[48,4096]{1,0:T(8,128)(2,1)} custom-call(bf16[48,4096]{1,0:T(8,128)(2,1)} %all_gather.3.near_ref, f32[8,1024]{1,0:T(8,128)} %broadcast_bitcast_fusion.digits_ref), custom_call_target="tpu_custom_call" | custom-call | tf_op jit(solution)/shard_map/pallas_call | solution.py:241
  22.0 3.9 %collective-permute-start.4 = (bf16[48,4096]{1,0:T(8,128)(2,1)}, bf16[48,4096]{1,0:T(8,128)(2,1)S(1)}, u32[]{:S(2)}, u32[]{:S(2)}) collective-permute-start(bf16[48,4096]{1,0:T(8,128)(2,1)} %shard_map.111.refs_0_), channel_id=1, source_target_pairs={{0,28},{4,0},{8,4},{12,8},{16,12},{20,16},{24,20},{28,24},{1,29},{... | collective-permute-start | bytes 1179656 | tf_op jit(solution)/shard_map/ppermute | solution.py:253
  28.0 1.0 copy-done
  29.0 12.6 %shard_map.112 = (f32[48,2048]{1,0:T(8,128)S(1)}, f32[8,8,128]{2,1,0:T(8,128)S(1)}) custom-call(s32[9]{0:T(128)S(1)} %pad.places_ref, s32[1,2048]{1,0:T(1,128)S(1)} %add_multiply_fusion.rows_ref, bf16[48,4096]{1,0:T(8,128)(2,1)S(1)} %copy-done), custom_call_target="tpu_custom_call" | custom-call | flops 12582912000 | bytes 393216 | tf_op jit(solution)/shard_map/pallas_call | solution.py:124
  42.4 2.7 %collective-permute-start.5 = (bf16[48,4096]{1,0:T(8,128)(2,1)S(1)}, bf16[48,4096]{1,0:T(8,128)(2,1)S(1)}, u32[]{:S(2)}, u32[]{:S(2)}) collective-permute-start(bf16[48,4096]{1,0:T(8,128)(2,1)S(1)} %collective-permute-done.4.refs_1_), channel_id=1, source_target_pairs={{0,28},{4,0},{8,4},{12,8},{16,12},{20,16},{24,20},{28,24},{1,29},{... | collective-permute-start | bytes 1179656 | tf_op jit(solution)/shard_map/ppermute | solution.py:257
  45.1 24.6 %shard_map.113 = (f32[48,2048]{1,0:T(8,128)S(1)}, f32[8,8,128]{2,1,0:T(8,128)S(1)}) custom-call(s32[9]{0:T(128)S(1)} %pad_add_fusion.3.places_ref, s32[1,2048]{1,0:T(1,128)S(1)} %add_multiply_fusion.rows_ref, bf16[48,4096]{1,0:T(8,128)(2,1)S(1)} %collective-permute-done.refs_0_, bf16[48,4096]{1,0:T(8,128)(2,1)S(1)} %collective-permute-done.4.refs_1_, ...), custom_call_target="tpu_custom_call" | custom-call | flops 25165824000 | bytes 786432 | tf_op jit(solution)/shard_map/pallas_call | solution.py:124
  69.8 2.7 %collective-permute-start.6 = (bf16[48,4096]{1,0:T(8,128)(2,1)S(1)}, bf16[48,4096]{1,0:T(8,128)(2,1)S(1)}, u32[]{:S(2)}, u32[]{:S(2)}) collective-permute-start(bf16[48,4096]{1,0:T(8,128)(2,1)S(1)} %collective-permute-done.5.refs_1_), channel_id=1, source_target_pairs={{0,28},{4,0},{8,4},{12,8},{16,12},{20,16},{24,20},{28,24},{1,29},{... | collective-permute-start | bytes 1179656 | tf_op jit(solution)/shard_map/ppermute | solution.py:257
  72.5 24.6 %shard_map.114 = (f32[48,2048]{1,0:T(8,128)S(1)}, f32[8,8,128]{2,1,0:T(8,128)S(1)}) custom-call(s32[9]{0:T(128)S(1)} %pad_add_fusion.2.places_ref, s32[1,2048]{1,0:T(1,128)S(1)} %add_multiply_fusion.rows_ref, bf16[48,4096]{1,0:T(8,128)(2,1)S(1)} %collective-permute-done.1.refs_0_, bf16[48,4096]{1,0:T(8,128)(2,1)S(1)} %collective-permute-done.5.refs_1_, ...), custom_call_target="tpu_custom_call" | custom-call | flops 25165824000 | bytes 786432 | tf_op jit(solution)/shard_map/pallas_call | solution.py:124
  97.2 24.6 %shard_map.115 = (f32[48,2048]{1,0:T(8,128)S(1)}, f32[8,8,128]{2,1,0:T(8,128)S(1)}) custom-call(s32[9]{0:T(128)S(1)} %pad_add_fusion.1.places_ref, s32[1,2048]{1,0:T(1,128)S(1)} %add_multiply_fusion.rows_ref, bf16[48,4096]{1,0:T(8,128)(2,1)S(1)} %collective-permute-done.2.refs_0_, bf16[48,4096]{1,0:T(8,128)(2,1)S(1)} %collective-permute-done.6.refs_1_, ...), custom_call_target="tpu_custom_call" | custom-call | flops 25165824000 | bytes 786432 | tf_op jit(solution)/shard_map/pallas_call | solution.py:124
  121.9 13.3 %shard_map.116 = (f32[48,2048]{1,0:T(8,128)S(1)}, f32[8,8,128]{2,1,0:T(8,128)}) custom-call(s32[9]{0:T(128)S(1)} %pad_add_fusion.places_ref, s32[1,2048]{1,0:T(1,128)S(1)} %add_multiply_fusion.rows_ref, bf16[48,4096]{1,0:T(8,128)(2,1)S(1)} %collective-permute-done.3.refs_0_, f32[48,2048]{1,0:T(8,128)S(1)} %get-tuple-element.26.refs_1_, ...), custom_call_target="tpu_custom_call" | custom-call | flops 12582912000 | bytes 393216 | tf_op jit(solution)/shard_map/pallas_call | solution.py:124
  135.2 1.4 collective-permute-start.7
  136.5 2.6 %collective-permute-start.8 = (f32[48,512]{1,0:T(8,128)S(1)}, f32[48,512]{1,0:T(8,128)S(1)}, u32[]{:S(2)}, u32[]{:S(2)}) collective-permute-start(f32[48,512]{1,0:T(8,128)S(1)} %get-tuple-element.42), channel_id=1, source_target_pairs={{0,2},{1,3},{2,0},{3,1},{4,6},{5,7},{6,4},{7,5},{8,10},{9,11},{10,... | collective-permute-start | bytes 294920 | tf_op jit(solution)/shard_map/ppermute | solution.py:267
  139.2 1.1 collective-permute-start.9
  140.8 1.6 collective-permute-done.8
  142.3 1.5 collective-permute-done.9
  143.8 0.8 pad_maximum_fusion.pieces_ref
  144.6 6.6 %shard_map.117 = (f32[1,512]{1,0:T(1,128)}, f32[32,512]{1,0:T(8,128)}, f32[8,128]{1,0:T(8,128)}, f32[32,32]{1,0:T(8,128)}) custom-call(s32[4]{0:T(128)} %and_select_fusion.4.order_ref, f32[4,48,512]{2,1,0:T(8,128)} %pad_maximum_fusion.pieces_ref), custom_call_target="tpu_custom_call" | custom-call | tf_op jit(solution)/shard_map/pallas_call | solution.py:274
  151.2 0.7 broadcast_in_dim.14
  151.9 10.3 %all_to_all.10 = f32[8,8,128]{2,1,0:T(8,128)S(1)} all-to-all(f32[8,8,128]{2,1,0:T(8,128)S(1)} %broadcast_in_dim.14), channel_id=1, replica_groups=mesh['x'=4,'core'=2,'z'=8,'y'=4] {'x','core'}, dimensions={0} | all-to-all | bytes 65536 | tf_op jit(solution)/shard_map/all_to_all | solution.py:223
  162.2 17.7 %all_to_all.11.grams_ref = f32[32,8,128]{2,1,0:T(8,128)} all-to-all(f32[32,8,128]{2,1,0:T(8,128)S(1)} %broadcast_in_dim.15), channel_id=1, replica_groups=mesh['x'=4,'core'=2,'z'=8,'y'=4] {'z','y'}, dimensions={0} | all-to-all | bytes 262144 | tf_op jit(solution)/shard_map/all_to_all | solution.py:223
  179.9 7.8 %shard_map.118 = (f32[32,512]{1,0:T(8,128)}, f32[32,32]{1,0:T(8,128)}, f32[32,32]{1,0:T(8,128)}) custom-call(f32[32,8,128]{2,1,0:T(8,128)} %all_to_all.11.grams_ref, f32[32,512]{1,0:T(8,128)} %get-tuple-element.30.scaled_ref, f32[32,32]{1,0:T(8,128)} %get-tuple-element.31.input_upper_ref), custom_call_target="tpu_custom_call" | custom-call | tf_op jit(solution)/shard_map/pallas_call | solution.py:284
  (48 shorter events, 4.3 us)
Async XLA Ops:
  1.5 1.0 copy-start.1
  1.7 0.7 copy-start.2
  21.7 20.6 %collective-permute-start = (bf16[48,4096]{1,0:T(8,128)(2,1)}, bf16[48,4096]{1,0:T(8,128)(2,1)S(1)}, u32[]{:S(2)}, u32[]{:S(2)}) collective-permute-start(bf16[48,4096]{1,0:T(8,128)(2,1)} %shard_map.111.refs_0_), channel_id=1, source_target_pairs={{0,4},{4,8},{8,12},{12,16},{16,20},{20,24},{24,28},{28,0},{1,5},{5... | collective-permute-start | bytes 1179656 | tf_op jit(solution)/shard_map/ppermute | solution.py:253
  22.0 20.4 %collective-permute-start.4 = (bf16[48,4096]{1,0:T(8,128)(2,1)}, bf16[48,4096]{1,0:T(8,128)(2,1)S(1)}, u32[]{:S(2)}, u32[]{:S(2)}) collective-permute-start(bf16[48,4096]{1,0:T(8,128)(2,1)} %shard_map.111.refs_0_), channel_id=1, source_target_pairs={{0,28},{4,0},{8,4},{12,8},{16,12},{20,16},{24,20},{28,24},{1,29},{... | collective-permute-start | bytes 1179656 | tf_op jit(solution)/shard_map/ppermute | solution.py:253
  25.9 0.7 copy-start.6
  26.7 0.7 copy-start.5
  27.3 0.7 copy-start.4
  28.0 1.0 copy-start
  41.6 0.7 copy-start.3
  42.4 27.3 %collective-permute-start.1 = (bf16[48,4096]{1,0:T(8,128)(2,1)S(1)}, bf16[48,4096]{1,0:T(8,128)(2,1)S(1)}, u32[]{:S(2)}, u32[]{:S(2)}) collective-permute-start(bf16[48,4096]{1,0:T(8,128)(2,1)S(1)} %collective-permute-done.refs_0_), channel_id=1, source_target_pairs={{0,4},{4,8},{8,12},{12,16},{16,20},{20,24},{24,28},{28,0},{1,5},{5... | collective-permute-start | bytes 1179656 | tf_op jit(solution)/shard_map/ppermute | solution.py:256
  42.4 27.4 %collective-permute-start.5 = (bf16[48,4096]{1,0:T(8,128)(2,1)S(1)}, bf16[48,4096]{1,0:T(8,128)(2,1)S(1)}, u32[]{:S(2)}, u32[]{:S(2)}) collective-permute-start(bf16[48,4096]{1,0:T(8,128)(2,1)S(1)} %collective-permute-done.4.refs_1_), channel_id=1, source_target_pairs={{0,28},{4,0},{8,4},{12,8},{16,12},{20,16},{24,20},{28,24},{1,29},{... | collective-permute-start | bytes 1179656 | tf_op jit(solution)/shard_map/ppermute | solution.py:257
  69.7 27.4 %collective-permute-start.2 = (bf16[48,4096]{1,0:T(8,128)(2,1)S(1)}, bf16[48,4096]{1,0:T(8,128)(2,1)S(1)}, u32[]{:S(2)}, u32[]{:S(2)}) collective-permute-start(bf16[48,4096]{1,0:T(8,128)(2,1)S(1)} %collective-permute-done.1.refs_0_), channel_id=1, source_target_pairs={{0,4},{4,8},{8,12},{12,16},{16,20},{20,24},{24,28},{28,0},{1,5},{5... | collective-permute-start | bytes 1179656 | tf_op jit(solution)/shard_map/ppermute | solution.py:256
  69.8 27.4 %collective-permute-start.6 = (bf16[48,4096]{1,0:T(8,128)(2,1)S(1)}, bf16[48,4096]{1,0:T(8,128)(2,1)S(1)}, u32[]{:S(2)}, u32[]{:S(2)}) collective-permute-start(bf16[48,4096]{1,0:T(8,128)(2,1)S(1)} %collective-permute-done.5.refs_1_), channel_id=1, source_target_pairs={{0,28},{4,0},{8,4},{12,8},{16,12},{20,16},{24,20},{28,24},{1,29},{... | collective-permute-start | bytes 1179656 | tf_op jit(solution)/shard_map/ppermute | solution.py:257
  97.1 24.8 %collective-permute-start.3 = (bf16[48,4096]{1,0:T(8,128)(2,1)S(1)}, bf16[48,4096]{1,0:T(8,128)(2,1)S(1)}, u32[]{:S(2)}, u32[]{:S(2)}) collective-permute-start(bf16[48,4096]{1,0:T(8,128)(2,1)S(1)} %collective-permute-done.2.refs_0_), channel_id=1, source_target_pairs={{0,4},{4,8},{8,12},{12,16},{16,20},{20,24},{24,28},{28,0},{1,5},{5... | collective-permute-start | bytes 1179656 | tf_op jit(solution)/shard_map/ppermute | solution.py:256
  135.2 5.6 %collective-permute-start.7 = (f32[48,512]{1,0:T(8,128)S(1)}, f32[48,512]{1,0:T(8,128)S(1)}, u32[]{:S(2)}, u32[]{:S(2)}) collective-permute-start(f32[48,512]{1,0:T(8,128)S(1)} %get-tuple-element.43), channel_id=1, source_target_pairs={{0,1},{1,2},{2,3},{3,0},{4,5},{5,6},{6,7},{7,4},{8,9},{9,10},{10,1... | collective-permute-start | bytes 294920 | tf_op jit(solution)/shard_map/ppermute | solution.py:267
  136.5 5.8 %collective-permute-start.8 = (f32[48,512]{1,0:T(8,128)S(1)}, f32[48,512]{1,0:T(8,128)S(1)}, u32[]{:S(2)}, u32[]{:S(2)}) collective-permute-start(f32[48,512]{1,0:T(8,128)S(1)} %get-tuple-element.42), channel_id=1, source_target_pairs={{0,2},{1,3},{2,0},{3,1},{4,6},{5,7},{6,4},{7,5},{8,10},{9,11},{10,... | collective-permute-start | bytes 294920 | tf_op jit(solution)/shard_map/ppermute | solution.py:267
  139.2 4.6 %collective-permute-start.9 = (f32[48,512]{1,0:T(8,128)S(1)}, f32[48,512]{1,0:T(8,128)S(1)}, u32[]{:S(2)}, u32[]{:S(2)}) collective-permute-start(f32[48,512]{1,0:T(8,128)S(1)} %get-tuple-element.41), channel_id=1, source_target_pairs={{0,3},{1,0},{2,1},{3,2},{4,7},{5,4},{6,5},{7,6},{8,11},{9,8},{10,9... | collective-permute-start | bytes 294920 | tf_op jit(solution)/shard_map/ppermute | solution.py:267

commit v5 on v4

v5 whole, which is shorter than its diff:
```python
import functools
import math

import jax
import jax.numpy as jnp
from jax import lax
from jax.experimental import pallas as pl
from jax.experimental.pallas import tpu as pltpu
from jax.sharding import Mesh
from jax.sharding import PartitionSpec as P

N = 131072
VECS = 32
PAD = 48
KEYCOLS = 256
X, CORE, Z, Y = 4, 2, 8, 4
OWN = N // (X * CORE * Z * Y)
ROWS = OWN * Y
SEG = OWN * X * CORE
GROUP = 32
SPARE = 40
GRAM_ROW = 40
LANES = 512
KEYS = SEG // KEYCOLS
GRAM_TILE = 4 * (KEYS // 8)
SCALE = 2.0 / math.sqrt(5461.25 * N)
HIGH = lax.Precision.HIGHEST
VMEM_LIMIT = 48 * 2**20
STEP = 16
X_AT, CORE_AT, Z_AT, Y_AT = range(4)
VMEM = pl.BlockSpec(memory_space=pltpu.VMEM)
SMEM = pl.BlockSpec(memory_space=pltpu.SMEM)


def shift_right(value, amount):
    return lax.shift_right_logical(value, jnp.full(value.shape, amount, jnp.int32))


def coupling(value):
    value = value ^ shift_right(value, 15)
    value = value * jnp.int32(739982445)
    value = value ^ shift_right(value, 13)
    value = value * jnp.int32(695872825)
    value = value ^ shift_right(value, 16)
    return (value.astype(jnp.int8) ^ jnp.int8(-128)).astype(jnp.bfloat16)


def spare_tile(block_ref, tile):
    return block_ref[SPARE - 8 : SPARE + 8, 128 * tile : 128 * tile + 128].astype(jnp.float32)[8:]


def pair_kernel(at_ref, tangent_ref, activity_ref, other_ref, pair_ref):
    rest = jnp.concatenate(
        (activity_ref[...].astype(jnp.float32), jnp.zeros((PAD - VECS - 1, OWN), jnp.float32))
    )
    here = pl.ds(pl.multiple_of(at_ref[CORE_AT] * OWN, OWN), OWN)
    there = pl.ds(pl.multiple_of((1 - at_ref[CORE_AT]) * OWN, OWN), OWN)
    pair_ref[:VECS, here] = tangent_ref[...]
    pair_ref[VECS:, here] = rest.astype(jnp.bfloat16)
    pair_ref[:, there] = other_ref[...]


def own_kernel(tangent_ref, activity_ref, own_ref):
    rest = jnp.concatenate(
        (activity_ref[...].astype(jnp.float32), jnp.zeros((PAD - VECS - 1, OWN), jnp.float32))
    )
    own_ref[:VECS, :] = tangent_ref[...]
    own_ref[VECS:, :] = rest.astype(jnp.bfloat16)


def block_kernel(at_ref, keys_ref, *refs):
    pair_refs, block_ref = refs[:X], refs[X]
    wide = CORE * OWN
    for shift in range(X):
        chip = lax.rem(at_ref[X_AT] + X - shift, X)
        block_ref[:, pl.ds(pl.multiple_of(chip * wide, wide), wide)] = pair_refs[shift][...]
    own = block_ref[:VECS, :]
    gram = lax.dot_general(own, own, (((1,), (1,)), ((), ())), preferred_element_type=jnp.float32)
    rest = pack_gram(gram / N)
    rows = lax.broadcasted_iota(jnp.int32, (8, 128), 0)
    parts = []
    for part in range(KEYS // 8):
        keys = jnp.zeros((8, 128), jnp.int32)
        for row in range(8):
            keys = jnp.where(rows == row, keys_ref[0, part * 8 + row], keys)
        parts.append(keys)
    tiles = []
    for digit in range(4):
        for keys in parts:
            tiles.append(jnp.bitwise_and(shift_right(keys, 8 * digit), 255).astype(jnp.float32))
    for _ in range(3):
        part = rest.astype(jnp.bfloat16).astype(jnp.float32)
        tiles.append(part)
        rest = rest - part
    for k, tile in enumerate(tiles):
        lanes = slice(128 * k, 128 * k + 128)
        above = block_ref[SPARE - 8 : SPARE + 8, lanes].astype(jnp.float32)[:8]
        block_ref[SPARE - 8 : SPARE + 8, lanes] = jnp.concatenate((above, tile)).astype(jnp.bfloat16)


def drive_kernel(at_ref, *refs, shifts, earlier):
    blocks = len(shifts)
    block_refs = refs[:blocks]
    earlier_refs = refs[blocks : blocks + 2 * earlier]
    out_ref, grams_ref, vectors_ref, bases_ref = refs[blocks + 2 * earlier :]
    groups = SEG // GROUP

    for slot in range(Z):
        grams_ref[slot] = earlier_refs[1][slot] if earlier else jnp.zeros((8, 128), jnp.float32)
    steps = lax.broadcasted_iota(jnp.int32, (8, 128), 0) * jnp.int32(GROUP)
    for k, shift in enumerate(shifts):
        place = lax.rem(at_ref[Z_AT] + (Z + shift), Z)
        vectors_ref[k] = block_refs[k][...]
        gram = jnp.zeros((8, 128), jnp.float32)
        for part in range(3):
            gram = gram + spare_tile(block_refs[k], GRAM_TILE + part)
        grams_ref[place] = gram
        first_column = (place * Y + at_ref[Y_AT]) * SEG
        for part in range(KEYS // 8):
            keys = jnp.zeros((8, 128), jnp.int32)
            for digit in range(4):
                tile = spare_tile(block_refs[k], digit * (KEYS // 8) + part)
                keys = keys + tile.astype(jnp.int32) * jnp.int32(256**digit)
            for row in range(8):
                key = part * 8 + row
                columns = first_column + key * KEYCOLS + steps
                at = k * groups + key * 8
                bases_ref[at : at + 8, :] = keys[row : row + 1] + columns * jnp.int32(668265261)

    first_row = (at_ref[X_AT] * CORE + at_ref[CORE_AT]) * (N // (X * CORE)) + at_ref[Z_AT] * ROWS
    row_at = lax.broadcasted_iota(jnp.int32, (GROUP, 128), 1)
    spread = lax.broadcasted_iota(jnp.int32, (GROUP, 128), 0) * jnp.int32(668265261)

    def lanes_body(part, carry):
        lane = pl.multiple_of(part * LANES, LANES)
        starts = [
            (first_row + lane + 128 * k + row_at) * jnp.int32(374761393) + spread
            for k in range(LANES // 128)
        ]

        def body(number, total):
            first = pl.multiple_of(number * groups, groups)
            parts = []
            for group in range(groups):
                base = bases_ref[pl.ds(first + group, 1), :]
                parts.append(jnp.concatenate([coupling(base + start) for start in starts], axis=1))
            return total + jnp.dot(
                vectors_ref[number],
                jnp.concatenate(parts, axis=0),
                preferred_element_type=jnp.float32,
            )

        here = pl.ds(lane, LANES)
        initial = earlier_refs[0][:, here] if earlier else jnp.zeros((PAD, LANES), jnp.float32)
        out_ref[:, here] = lax.fori_loop(0, blocks, body, initial)
        return carry

    lax.fori_loop(0, ROWS // LANES, lanes_body, 0)
    gram = grams_ref[0]
    for slot in range(1, Z):
        gram = gram + grams_ref[slot]
    for part in range(Y):
        out_ref[GRAM_ROW:, part * OWN : part * OWN + 128] = gram


def partial_drive(at, shifts, blocks, earlier=()):
    count = len(blocks)
    return pl.pallas_call(
        functools.partial(drive_kernel, shifts=shifts, earlier=len(earlier) // 2),
        in_specs=[SMEM] + [VMEM] * (count + len(earlier)),
        out_specs=(VMEM, VMEM),
        out_shape=(
            jax.ShapeDtypeStruct((PAD, ROWS), jnp.float32),
            jax.ShapeDtypeStruct((Z, 8, 128), jnp.float32),
        ),
        scratch_shapes=[
            pltpu.VMEM((count, PAD, SEG), jnp.bfloat16),
            pltpu.VMEM((count * SEG // GROUP, 128), jnp.int32),
        ],
        cost_estimate=pl.CostEstimate(
            flops=count * SEG * ROWS * 1500, bytes_accessed=count * PAD * SEG * 2, transcendentals=0
        ),
        compiler_params=pltpu.CompilerParams(vmem_limit_bytes=VMEM_LIMIT),
    )(at, *blocks, *earlier)


def pack_gram(gram):
    return jnp.concatenate([gram[8 * k : 8 * k + 8] for k in range(4)], axis=1)


def unpack_gram(packed):
    return jnp.concatenate([packed[:, 32 * k : 32 * k + 32] for k in range(4)], axis=0)


def gram_of(rows):
    return lax.dot_general(
        rows, rows, (((1,), (1,)), ((), ())), precision=HIGH, preferred_element_type=jnp.float32
    ) / N


def dot(left, right):
    return jnp.dot(left, right, precision=HIGH, preferred_element_type=jnp.float32)


def factor(gram, floor=0.0):
    rows = lax.broadcasted_iota(jnp.int32, (VECS, VECS), 0)
    columns = lax.broadcasted_iota(jnp.int32, (VECS, VECS), 1)
    wide = (VECS, 2 * VECS)
    row_at = lax.broadcasted_iota(jnp.int32, wide, 0)
    work = jnp.concatenate((gram, (rows == columns).astype(jnp.float32)), axis=1)
    scales = jnp.zeros(wide, jnp.float32)
    for first in range(0, VECS, STEP):
        spread = [
            jnp.broadcast_to(work[:, first + k : first + k + 1], wide) for k in range(STEP)
        ]
        ratios = []
        for k in range(STEP):
            at = first + k
            column = spread[k]
            for m in range(k):
                element = jnp.broadcast_to(column[first + m : first + m + 1], wide)
                column = column - ratios[m] * element
            pivot = jnp.broadcast_to(column[at : at + 1], wide)
            if floor:
                least = jnp.maximum(floor * gram[at : at + 1, at : at + 1], 1e-30)
                pivot = jnp.maximum(pivot, least)
            ratios.append(jnp.where(row_at > at, column / pivot, 0.0))
            scales = jnp.where(row_at == at, lax.rsqrt(pivot), scales)
        for k in range(STEP):
            work = work - ratios[k] * jnp.broadcast_to(work[first + k : first + k + 1], wide)
    diagonal = jnp.where(rows == columns, 1.0 / scales[:, :VECS], 0.0)
    work = work * scales
    upper = jnp.where(rows < columns, work[:, :VECS], diagonal)
    return upper, work[:, VECS:]


def first_kernel(at_ref, mine_ref, others_ref, *refs):
    others_ref, refs = (others_ref, *refs[: Y - 2]), refs[Y - 2 :]
    state_ref, scaled_ref, gram_ref, upper_ref, inputs_ref = refs
    drive = mine_ref[...]
    inputs_ref[at_ref[Y_AT]] = drive[GRAM_ROW:, :128]
    for shift, other_ref in enumerate(others_ref, 1):
        drive = drive + other_ref[...]
        inputs_ref[lax.rem(at_ref[Y_AT] + (Y - shift), Y)] = other_ref[GRAM_ROW:, :128]
    state = jnp.tanh(SCALE * drive[VECS : VECS + 1])
    grown = (SCALE * (1.0 - state * state)) * drive[:VECS]
    inputs = inputs_ref[0]
    for k in range(1, Y):
        inputs = inputs + inputs_ref[k]
    upper, inverse = factor(unpack_gram(inputs), 1e-6)
    scaled = dot(inverse, grown)
    state_ref[...] = state
    scaled_ref[...] = scaled
    gram_ref[...] = pack_gram(gram_of(scaled))
    upper_ref[...] = upper


def second_kernel(grams_ref, scaled_ref, input_upper_ref, result_ref, product_ref, upper_ref):
    gram = unpack_gram(jnp.sum(grams_ref[...], axis=0))
    near_upper, inverse = factor(gram)
    first = dot(inverse, scaled_ref[...])
    upper = dot(near_upper, input_upper_ref[...])
    gram_two = lax.dot_general(
        dot(inverse, gram),
        inverse,
        (((1,), (1,)), ((), ())),
        precision=HIGH,
        preferred_element_type=jnp.float32,
    )
    second_upper, second_inverse = factor(gram_two)
    result_ref[...] = dot(second_inverse, first)
    product_ref[...] = dot(second_upper, upper)
    upper_ref[...] = upper


def spread_to(value, axes, count):
    return lax.all_to_all(jnp.broadcast_to(value, (count, *value.shape)), axes, 0, 0)


def gather_grams(gram):
    near = jnp.sum(spread_to(gram, ("x", "core"), X * CORE), axis=0)
    return spread_to(near, ("z", "y"), Z * Y)


def per_device(tangent, activity, block_keys):
    y = lax.axis_index("y")
    at = jnp.stack([lax.axis_index(axis) for axis in ("x", "core", "z", "y")]).astype(jnp.int32)
    activity = activity.reshape(1, -1)
    block = jax.ShapeDtypeStruct((PAD, OWN), jnp.bfloat16)
    own = pl.pallas_call(own_kernel, out_shape=block)(tangent, activity)
    other = lax.ppermute(own, "core", [(0, 1), (1, 0)])
    pair = pl.pallas_call(
        pair_kernel,
        in_specs=[SMEM, VMEM, VMEM, VMEM],
        out_shape=jax.ShapeDtypeStruct((PAD, CORE * OWN), jnp.bfloat16),
    )(at, tangent, activity, other)
    pairs = [pair] + [
        lax.ppermute(pair, "x", [(i, (i + shift) % X) for i in range(X)]) for shift in range(1, X)
    ]
    near = pl.pallas_call(
        block_kernel,
        in_specs=[SMEM, SMEM] + [VMEM] * X,
        out_shape=jax.ShapeDtypeStruct((PAD, SEG), jnp.bfloat16),
    )(at, block_keys, *pairs)

    up = [(i, (i + 1) % Z) for i in range(Z)]
    down = [(i, (i - 1) % Z) for i in range(Z)]
    below, above = lax.ppermute(near, "z", up), lax.ppermute(near, "z", down)
    earlier = partial_drive(at, (0,), [near])
    for step in range(1, Z // 2):
        next_below = lax.ppermute(below, "z", up)
        next_above = lax.ppermute(above, "z", down) if step + 1 < Z // 2 else None
        earlier = partial_drive(at, (-step, step), [below, above], earlier)
        below, above = next_below, next_above
    partial, _ = partial_drive(at, (Z // 2,), [below], earlier)

    pieces = []
    for shift in range(Y):
        to = (y + shift) % Y
        piece = lax.dynamic_slice_in_dim(partial, to * OWN, OWN, 1)
        if shift:
            piece = lax.ppermute(piece, "y", [(i, (i + shift) % Y) for i in range(Y)])
        pieces.append(piece)

    square = jax.ShapeDtypeStruct((VECS, VECS), jnp.float32)
    wide = jax.ShapeDtypeStruct((VECS, OWN), jnp.float32)
    state, scaled, gram, input_upper = pl.pallas_call(
        first_kernel,
        in_specs=[SMEM] + [VMEM] * Y,
        out_shape=(
            jax.ShapeDtypeStruct((1, OWN), jnp.float32),
            wide,
            jax.ShapeDtypeStruct((8, 128), jnp.float32),
            square,
        ),
        scratch_shapes=[pltpu.VMEM((Y, 8, 128), jnp.float32)],
    )(at, *pieces)
    result, product, upper = pl.pallas_call(second_kernel, out_shape=(wide, square, square))(
        gather_grams(gram), scaled, input_upper
    )
    return result, state.reshape(OWN), product, upper


def solution(mesh):
    split = Mesh(mesh.devices.reshape(X, CORE, Z, Y), ("x", "core", "z", "y"))
    columns, rows = ("z", "y", "x", "core"), ("x", "core", "z", "y")
    return jax.shard_map(
        per_device,
        mesh=split,
        in_specs=(P(None, columns), P(columns), P(("x", "core"), ("z", "y"))),
        out_specs=(P(None, rows), P(rows), P(), P()),
        check_vma=False,
    )
```

time: 188 us -> 177 us (0.941)
  blocking collectives: 45.2 us -> 29.5 us
  starting transfers between devices: 14.7 us -> 22.3 us
  Pallas kernels: 116 us -> 110 us
  waiting for transfers between devices: 3.06 us -> 7.86 us
    all_gather x1 -> x0, blocking collectives: 17.2 us -> none  [per_device(): near = lax.all_gather(own, ('x', 'core'), axis=1, tiled=True)]
    ppermute x0 -> x4, starting transfers between devices: none -> 6.32 us  [the longest x1 3.24 us: per_device(): other = lax.ppermute(own, 'core', [(0, 1), (1, 0)])]
    ppermute x0 -> x4, waiting for transfers between devices: none -> 5.16 us  [the longest x3 4.73 us: per_device(): lax.ppermute(pair, 'x', [(i, (i + shift) % X) for i in range(X)])]
    pallas_call x1, Pallas kernels: 7.85 us -> 3.64 us  [per_device(): pl.pallas_call(second_kernel, out_shape=(wide, square, square))]
    pallas_call x7 -> x9, Pallas kernels: 108 us -> 106 us  [the longest x5 98.4 us: partial_drive(): pl.pallas_call(functools.partial(drive_kernel, shifts=shifts, earlier=len...]
  transfers between devices with their start and end apart: 10 -> 14, of which waited for: 2 -> 6; matrix products, arithmetic and copies ran while one was open for 1% -> 0% of each run, Pallas kernels for 46% -> 49%
where the time goes in v5:
time: 177 us
  Pallas kernels  110 us (62%)
  blocking collectives  29.5 us (17%)
  starting transfers between devices  22.3 us (13%)
  waiting for transfers between devices  7.86 us (4%)
  local copies, waits for them, and re-layouts  5.59 us (3%)
    pallas_call x5, Pallas kernels, partial_drive(): pl.pallas_call(functools.partial(drive_kernel, shifts=shifts, earlier=len...  98.4 us
    all_to_all x2, blocking collectives, spread_to(): lax.all_to_all(jnp.broadcast_to(value, (count, *value.shape)), axes, 0, 0)  29.5 us
    ppermute x2, starting transfers between devices, per_device(): next_above = lax.ppermute(above, 'z', down) if step + 1 < Z // 2 else None  5.31 us
    ppermute x2, starting transfers between devices, per_device(): below, above = (lax.ppermute(near, 'z', up), lax.ppermute(near, 'z', down))  5.2 us
    ppermute x3, starting transfers between devices, per_device(): piece = lax.ppermute(piece, 'y', [(i, (i + shift) % Y) for i in range(Y)])  4.98 us
    ppermute x3, waiting for transfers between devices, per_device(): lax.ppermute(pair, 'x', [(i, (i + shift) % X) for i in range(X)])  4.73 us
    pallas_call x1, Pallas kernels, per_device(): pl.pallas_call(second_kernel, out_shape=(wide, square, square))  3.64 us
  transfers between devices with their start and end apart: 14, of which 6 were waited for; matrix products, arithmetic and copies ran while one was open for 0% of the time, Pallas kernels for 49%

profile of v5, /device:TPU:1, one launch (start us, length us, event | category | flops | bytes accessed | tf_op | source)
XLA Modules:
  0.0 176.7 jit_solution(6421090339103463334)
XLA Ops:
  0.6 1.3 reshape.14.activity_ref
  1.9 1.4 shard_map.66
  3.3 3.2 %collective-permute-start = (bf16[48,512]{1,0:T(8,128)(2,1)}, bf16[48,512]{1,0:T(8,128)(2,1)S(1)}, u32[]{:S(2)}, u32[]{:S(2)}) collective-permute-start(bf16[48,512]{1,0:T(8,128)(2,1)} %shard_map.66), channel_id=1, source_target_pairs={{0,32},{32,0},{1,33},{33,1},{2,34},{34,2},{3,35},{35,3},{4,36},{36... | collective-permute-start | bytes 147464 | tf_op jit(solution)/shard_map/ppermute | solution.py:291
  8.2 1.5 shard_map.67.refs_0_
  9.7 1.9 %collective-permute-start.2 = (bf16[48,1024]{1,0:T(8,128)(2,1)}, bf16[48,1024]{1,0:T(8,128)(2,1)S(1)}, u32[]{:S(2)}, u32[]{:S(2)}) collective-permute-start(bf16[48,1024]{1,0:T(8,128)(2,1)} %shard_map.67.refs_0_), channel_id=1, source_target_pairs={{0,128},{64,192},{128,0},{192,64},{1,129},{65,193},{129,1},{193,65... | collective-permute-start | bytes 294920 | tf_op jit(solution)/shard_map/ppermute | solution.py:298
  11.6 1.2 collective-permute-start.3
  12.8 3.3 %collective-permute-done.1.refs_1_ = bf16[48,1024]{1,0:T(8,128)(2,1)S(1)} collective-permute-done((bf16[48,1024]{1,0:T(8,128)(2,1)}, bf16[48,1024]{1,0:T(8,128)(2,1)S(1)}, u32[]{:S(2)}, u32[]{:S(2)}) %collective-permute-start.1) | collective-permute-done | bytes 98336 | tf_op jit(solution)/shard_map/ppermute | solution.py:298
  18.2 2.1 %shard_map.68.refs_0_ = bf16[48,4096]{1,0:T(8,128)(2,1)} custom-call(s32[4]{0:T(128)} %pad_add_fusion.at_ref, s32[1,16]{1,0:T(1,128)} %keys_ref.1, bf16[48,1024]{1,0:T(8,128)(2,1)} %shard_map.67.refs_0_, bf16[48,1024]{1,0:T(8,128)(2,1)} %copy-done.2, bf16[48,1024]{1,0:T(8,128)(2,1)} %copy-done.3, bf16[48,1024]{1,0:T(8,128)(2,1)} %copy-done.4), custom_call_target="tpu_custom_call" | custom-call | tf_op jit(solution)/shard_map/pallas_call | solution.py:300
  20.3 1.3 collective-permute-start.4
  21.6 3.9 %collective-permute-start.8 = (bf16[48,4096]{1,0:T(8,128)(2,1)}, bf16[48,4096]{1,0:T(8,128)(2,1)S(1)}, u32[]{:S(2)}, u32[]{:S(2)}) collective-permute-start(bf16[48,4096]{1,0:T(8,128)(2,1)} %shard_map.68.refs_0_), channel_id=1, source_target_pairs={{0,28},{4,0},{8,4},{12,8},{16,12},{20,16},{24,20},{28,24},{1,29},{... | collective-permute-start | bytes 1179656 | tf_op jit(solution)/shard_map/ppermute | solution.py:308
  26.5 12.5 %shard_map.69 = (f32[48,2048]{1,0:T(8,128)S(1)}, f32[8,8,128]{2,1,0:T(8,128)S(1)}) custom-call(s32[4]{0:T(128)S(1)} %copy-done.1, bf16[48,4096]{1,0:T(8,128)(2,1)S(1)} %copy-done), custom_call_target="tpu_custom_call" | custom-call | flops 12582912000 | bytes 393216 | tf_op jit(solution)/shard_map/pallas_call | solution.py:168
  39.1 2.7 %collective-permute-start.9 = (bf16[48,4096]{1,0:T(8,128)(2,1)S(1)}, bf16[48,4096]{1,0:T(8,128)(2,1)S(1)}, u32[]{:S(2)}, u32[]{:S(2)}) collective-permute-start(bf16[48,4096]{1,0:T(8,128)(2,1)S(1)} %collective-permute-done.8.refs_1_), channel_id=1, source_target_pairs={{0,28},{4,0},{8,4},{12,8},{16,12},{20,16},{24,20},{28,24},{1,29},{... | collective-permute-start | bytes 1179656 | tf_op jit(solution)/shard_map/ppermute | solution.py:312
  41.8 24.5 %shard_map.70 = (f32[48,2048]{1,0:T(8,128)S(1)}, f32[8,8,128]{2,1,0:T(8,128)S(1)}) custom-call(s32[4]{0:T(128)S(1)} %copy-done.1, bf16[48,4096]{1,0:T(8,128)(2,1)S(1)} %collective-permute-done.4.refs_0_, bf16[48,4096]{1,0:T(8,128)(2,1)S(1)} %collective-permute-done.8.refs_1_, f32[48,2048]{1,0:T(8,128)S(1)} %get-tuple-element.20.refs_2_, ...), custom_call_target="tpu_custom_call" | custom-call | flops 25165824000 | bytes 786432 | tf_op jit(solution)/shard_map/pallas_call | solution.py:168
  66.4 2.7 %collective-permute-start.10 = (bf16[48,4096]{1,0:T(8,128)(2,1)S(1)}, bf16[48,4096]{1,0:T(8,128)(2,1)S(1)}, u32[]{:S(2)}, u32[]{:S(2)}) collective-permute-start(bf16[48,4096]{1,0:T(8,128)(2,1)S(1)} %collective-permute-done.9.refs_1_), channel_id=1, source_target_pairs={{0,28},{4,0},{8,4},{12,8},{16,12},{20,16},{24,20},{28,24},{1,29},{... | collective-permute-start | bytes 1179656 | tf_op jit(solution)/shard_map/ppermute | solution.py:312
  69.0 24.5 %shard_map.71 = (f32[48,2048]{1,0:T(8,128)S(1)}, f32[8,8,128]{2,1,0:T(8,128)S(1)}) custom-call(s32[4]{0:T(128)S(1)} %copy-done.1, bf16[48,4096]{1,0:T(8,128)(2,1)S(1)} %collective-permute-done.5.refs_0_, bf16[48,4096]{1,0:T(8,128)(2,1)S(1)} %collective-permute-done.9.refs_1_, f32[48,2048]{1,0:T(8,128)S(1)} %get-tuple-element.22.refs_2_, ...), custom_call_target="tpu_custom_call" | custom-call | flops 25165824000 | bytes 786432 | tf_op jit(solution)/shard_map/pallas_call | solution.py:168
  93.9 24.5 %shard_map.72 = (f32[48,2048]{1,0:T(8,128)S(1)}, f32[8,8,128]{2,1,0:T(8,128)S(1)}) custom-call(s32[4]{0:T(128)S(1)} %copy-done.1, bf16[48,4096]{1,0:T(8,128)(2,1)S(1)} %collective-permute-done.6.refs_0_, bf16[48,4096]{1,0:T(8,128)(2,1)S(1)} %collective-permute-done.10.refs_1_, f32[48,2048]{1,0:T(8,128)S(1)} %get-tuple-element.24.refs_2_, ...), custom_call_target="tpu_custom_call" | custom-call | flops 25165824000 | bytes 786432 | tf_op jit(solution)/shard_map/pallas_call | solution.py:168
  118.3 12.5 %shard_map.73 = (f32[48,2048]{1,0:T(8,128)S(1)}, f32[8,8,128]{2,1,0:T(8,128)}) custom-call(s32[4]{0:T(128)S(1)} %copy-done.1, bf16[48,4096]{1,0:T(8,128)(2,1)S(1)} %collective-permute-done.7.refs_0_, f32[48,2048]{1,0:T(8,128)S(1)} %get-tuple-element.26.refs_1_, f32[8,8,128]{2,1,0:T(8,128)S(1)} %get-tuple-element.27.refs_2_), custom_call_target="tpu_custom_call" | custom-call | flops 12582912000 | bytes 393216 | tf_op jit(solution)/shard_map/pallas_call | solution.py:168
  131.5 1.3 collective-permute-start.11
  132.8 2.6 %collective-permute-start.12 = (f32[48,512]{1,0:T(8,128)S(1)}, f32[48,512]{1,0:T(8,128)S(1)}, u32[]{:S(2)}, u32[]{:S(2)}) collective-permute-start(f32[48,512]{1,0:T(8,128)S(1)} %get-tuple-element.37), channel_id=1, source_target_pairs={{0,2},{1,3},{2,0},{3,1},{4,6},{5,7},{6,4},{7,5},{8,10},{9,11},{10,... | collective-permute-start | bytes 294920 | tf_op jit(solution)/shard_map/ppermute | solution.py:322
  136.5 2.0 %collective-permute-done.12.refs_0_ = f32[48,512]{1,0:T(8,128)S(1)} collective-permute-done((f32[48,512]{1,0:T(8,128)S(1)}, f32[48,512]{1,0:T(8,128)S(1)}, u32[]{:S(2)}, u32[]{:S(2)}) %collective-permute-start.12) | collective-permute-done | bytes 98336 | tf_op jit(solution)/shard_map/ppermute | solution.py:322
  139.9 2.9 %shard_map.74 = (f32[1,512]{1,0:T(1,128)}, f32[32,512]{1,0:T(8,128)}, f32[8,128]{1,0:T(8,128)}, f32[32,32]{1,0:T(8,128)}) custom-call(s32[4]{0:T(128)} %pad_add_fusion.at_ref, f32[48,512]{1,0:T(8,128)} %get-tuple-element.39.mine_ref, f32[48,512]{1,0:T(8,128)} %copy-done.5, f32[48,512]{1,0:T(8,128)} %copy-done.6, f32[48,512]{1,0:T(8,128)} %copy-done.7), custom_call_target="tpu_custom_call" | custom-call | tf_op jit(solution)/shard_map/pallas_call | solution.py:327
  143.5 11.8 %all_to_all.10 = f32[8,8,128]{2,1,0:T(8,128)S(1)} all-to-all(f32[8,8,128]{2,1,0:T(8,128)S(1)} %broadcast_in_dim.6), channel_id=1, replica_groups=mesh['x'=4,'core'=2,'z'=8,'y'=4] {'x','core'}, dimensions={0} | all-to-all | bytes 65536 | tf_op jit(solution)/shard_map/all_to_all | solution.py:277
  155.3 17.7 %all_to_all.11.grams_ref = f32[32,8,128]{2,1,0:T(8,128)} all-to-all(f32[32,8,128]{2,1,0:T(8,128)S(1)} %broadcast_in_dim.7), channel_id=1, replica_groups=mesh['x'=4,'core'=2,'z'=8,'y'=4] {'z','y'}, dimensions={0} | all-to-all | bytes 262144 | tf_op jit(solution)/shard_map/all_to_all | solution.py:277
  173.1 3.6 %shard_map.75 = (f32[32,512]{1,0:T(8,128)}, f32[32,32]{1,0:T(8,128)}, f32[32,32]{1,0:T(8,128)}) custom-call(f32[32,8,128]{2,1,0:T(8,128)} %all_to_all.11.grams_ref, f32[32,512]{1,0:T(8,128)} %get-tuple-element.30.scaled_ref, f32[32,32]{1,0:T(8,128)} %get-tuple-element.31.input_upper_ref), custom_call_target="tpu_custom_call" | custom-call | tf_op jit(solution)/shard_map/pallas_call | solution.py:338
  (40 shorter events, 9.1 us)
Async XLA Ops:
  3.3 4.3 %collective-permute-start = (bf16[48,512]{1,0:T(8,128)(2,1)}, bf16[48,512]{1,0:T(8,128)(2,1)S(1)}, u32[]{:S(2)}, u32[]{:S(2)}) collective-permute-start(bf16[48,512]{1,0:T(8,128)(2,1)} %shard_map.66), channel_id=1, source_target_pairs={{0,32},{32,0},{1,33},{33,1},{2,34},{34,2},{3,35},{35,3},{4,36},{36... | collective-permute-start | bytes 147464 | tf_op jit(solution)/shard_map/ppermute | solution.py:291
  7.6 0.6 copy-start.8
  9.7 6.4 %collective-permute-start.1 = (bf16[48,1024]{1,0:T(8,128)(2,1)}, bf16[48,1024]{1,0:T(8,128)(2,1)S(1)}, u32[]{:S(2)}, u32[]{:S(2)}) collective-permute-start(bf16[48,1024]{1,0:T(8,128)(2,1)} %shard_map.67.refs_0_), channel_id=1, source_target_pairs={{0,64},{64,128},{128,192},{192,0},{1,65},{65,129},{129,193},{193,1... | collective-permute-start | bytes 294920 | tf_op jit(solution)/shard_map/ppermute | solution.py:298
  9.7 6.8 %collective-permute-start.2 = (bf16[48,1024]{1,0:T(8,128)(2,1)}, bf16[48,1024]{1,0:T(8,128)(2,1)S(1)}, u32[]{:S(2)}, u32[]{:S(2)}) collective-permute-start(bf16[48,1024]{1,0:T(8,128)(2,1)} %shard_map.67.refs_0_), channel_id=1, source_target_pairs={{0,128},{64,192},{128,0},{192,64},{1,129},{65,193},{129,1},{193,65... | collective-permute-start | bytes 294920 | tf_op jit(solution)/shard_map/ppermute | solution.py:298
  11.6 5.9 %collective-permute-start.3 = (bf16[48,1024]{1,0:T(8,128)(2,1)}, bf16[48,1024]{1,0:T(8,128)(2,1)S(1)}, u32[]{:S(2)}, u32[]{:S(2)}) collective-permute-start(bf16[48,1024]{1,0:T(8,128)(2,1)} %shard_map.67.refs_0_), channel_id=1, source_target_pairs={{0,192},{64,0},{128,64},{192,128},{1,193},{65,1},{129,65},{193,129... | collective-permute-start | bytes 294920 | tf_op jit(solution)/shard_map/ppermute | solution.py:298
  12.8 12.7 %copy-start.1 = (s32[4]{0:T(128)S(1)}, s32[4]{0:T(128)}, u32[]{:S(2)}) copy-start(s32[4]{0:T(128)} %pad_add_fusion.at_ref) | copy-start | bytes 52
  16.1 1.5 copy-start.2
  16.5 1.0 copy-start.3
  17.5 0.6 copy-start.4
  20.3 18.7 %collective-permute-start.4 = (bf16[48,4096]{1,0:T(8,128)(2,1)}, bf16[48,4096]{1,0:T(8,128)(2,1)S(1)}, u32[]{:S(2)}, u32[]{:S(2)}) collective-permute-start(bf16[48,4096]{1,0:T(8,128)(2,1)} %shard_map.68.refs_0_), channel_id=1, source_target_pairs={{0,4},{4,8},{8,12},{12,16},{16,20},{20,24},{24,28},{28,0},{1,5},{5... | collective-permute-start | bytes 1179656 | tf_op jit(solution)/shard_map/ppermute | solution.py:308
  21.6 17.6 %collective-permute-start.8 = (bf16[48,4096]{1,0:T(8,128)(2,1)}, bf16[48,4096]{1,0:T(8,128)(2,1)S(1)}, u32[]{:S(2)}, u32[]{:S(2)}) collective-permute-start(bf16[48,4096]{1,0:T(8,128)(2,1)} %shard_map.68.refs_0_), channel_id=1, source_target_pairs={{0,28},{4,0},{8,4},{12,8},{16,12},{20,16},{24,20},{28,24},{1,29},{... | collective-permute-start | bytes 1179656 | tf_op jit(solution)/shard_map/ppermute | solution.py:308
  25.5 1.0 copy-start
  39.0 27.2 %collective-permute-start.5 = (bf16[48,4096]{1,0:T(8,128)(2,1)S(1)}, bf16[48,4096]{1,0:T(8,128)(2,1)S(1)}, u32[]{:S(2)}, u32[]{:S(2)}) collective-permute-start(bf16[48,4096]{1,0:T(8,128)(2,1)S(1)} %collective-permute-done.4.refs_0_), channel_id=1, source_target_pairs={{0,4},{4,8},{8,12},{12,16},{16,20},{20,24},{24,28},{28,0},{1,5},{5... | collective-permute-start | bytes 1179656 | tf_op jit(solution)/shard_map/ppermute | solution.py:311
  39.1 27.2 %collective-permute-start.9 = (bf16[48,4096]{1,0:T(8,128)(2,1)S(1)}, bf16[48,4096]{1,0:T(8,128)(2,1)S(1)}, u32[]{:S(2)}, u32[]{:S(2)}) collective-permute-start(bf16[48,4096]{1,0:T(8,128)(2,1)S(1)} %collective-permute-done.8.refs_1_), channel_id=1, source_target_pairs={{0,28},{4,0},{8,4},{12,8},{16,12},{20,16},{24,20},{28,24},{1,29},{... | collective-permute-start | bytes 1179656 | tf_op jit(solution)/shard_map/ppermute | solution.py:312
  66.3 27.2 %collective-permute-start.6 = (bf16[48,4096]{1,0:T(8,128)(2,1)S(1)}, bf16[48,4096]{1,0:T(8,128)(2,1)S(1)}, u32[]{:S(2)}, u32[]{:S(2)}) collective-permute-start(bf16[48,4096]{1,0:T(8,128)(2,1)S(1)} %collective-permute-done.5.refs_0_), channel_id=1, source_target_pairs={{0,4},{4,8},{8,12},{12,16},{16,20},{20,24},{24,28},{28,0},{1,5},{5... | collective-permute-start | bytes 1179656 | tf_op jit(solution)/shard_map/ppermute | solution.py:311
  66.4 27.5 %collective-permute-start.10 = (bf16[48,4096]{1,0:T(8,128)(2,1)S(1)}, bf16[48,4096]{1,0:T(8,128)(2,1)S(1)}, u32[]{:S(2)}, u32[]{:S(2)}) collective-permute-start(bf16[48,4096]{1,0:T(8,128)(2,1)S(1)} %collective-permute-done.9.refs_1_), channel_id=1, source_target_pairs={{0,28},{4,0},{8,4},{12,8},{16,12},{20,16},{24,20},{28,24},{1,29},{... | collective-permute-start | bytes 1179656 | tf_op jit(solution)/shard_map/ppermute | solution.py:312
  93.5 24.8 %collective-permute-start.7 = (bf16[48,4096]{1,0:T(8,128)(2,1)S(1)}, bf16[48,4096]{1,0:T(8,128)(2,1)S(1)}, u32[]{:S(2)}, u32[]{:S(2)}) collective-permute-start(bf16[48,4096]{1,0:T(8,128)(2,1)S(1)} %collective-permute-done.6.refs_0_), channel_id=1, source_target_pairs={{0,4},{4,8},{8,12},{12,16},{16,20},{20,24},{24,28},{28,0},{1,5},{5... | collective-permute-start | bytes 1179656 | tf_op jit(solution)/shard_map/ppermute | solution.py:311
  131.5 5.0 %collective-permute-start.11 = (f32[48,512]{1,0:T(8,128)S(1)}, f32[48,512]{1,0:T(8,128)S(1)}, u32[]{:S(2)}, u32[]{:S(2)}) collective-permute-start(f32[48,512]{1,0:T(8,128)S(1)} %get-tuple-element.38), channel_id=1, source_target_pairs={{0,1},{1,2},{2,3},{3,0},{4,5},{5,6},{6,7},{7,4},{8,9},{9,10},{10,1... | collective-permute-start | bytes 294920 | tf_op jit(solution)/shard_map/ppermute | solution.py:322
  132.8 5.7 %collective-permute-start.12 = (f32[48,512]{1,0:T(8,128)S(1)}, f32[48,512]{1,0:T(8,128)S(1)}, u32[]{:S(2)}, u32[]{:S(2)}) collective-permute-start(f32[48,512]{1,0:T(8,128)S(1)} %get-tuple-element.37), channel_id=1, source_target_pairs={{0,2},{1,3},{2,0},{3,1},{4,6},{5,7},{6,4},{7,5},{8,10},{9,11},{10,... | collective-permute-start | bytes 294920 | tf_op jit(solution)/shard_map/ppermute | solution.py:322
  135.5 3.8 %collective-permute-start.13 = (f32[48,512]{1,0:T(8,128)S(1)}, f32[48,512]{1,0:T(8,128)S(1)}, u32[]{:S(2)}, u32[]{:S(2)}) collective-permute-start(f32[48,512]{1,0:T(8,128)S(1)} %get-tuple-element.36), channel_id=1, source_target_pairs={{0,3},{1,0},{2,1},{3,2},{4,7},{5,4},{6,5},{7,6},{8,11},{9,8},{10,9... | collective-permute-start | bytes 294920 | tf_op jit(solution)/shard_map/ppermute | solution.py:322
  136.5 2.7 %copy-start.5 = (f32[48,512]{1,0:T(8,128)}, f32[48,512]{1,0:T(8,128)S(1)}, u32[]{:S(2)}) copy-start(f32[48,512]{1,0:T(8,128)S(1)} %collective-permute-done.11.others_ref) | copy-start | bytes 294916
  138.5 0.7 copy-start.6
  139.2 0.6 copy-start.7
